TPU v7x, 128 devices: a whole 4x4x4 slice. The times are simulated.
128 devices in a mesh: az: 8 (over z, x_lo), rg: 16 (over x_hi, y, core).
Axes of the slice: x: 4 (x_hi: 2, x_lo: 2; x = x_hi * 2 + x_lo), y: 4, z: 4, core: 2. Of those that a mesh axis runs over, the one named last changes fastest.
Arguments:
- echo: float32 [2, 2048, 4096], P(None, 'az', 'rg'), may hold values from -6 to 6
- range_row: int32 [4096], replicated, may hold values from 0 to 63
- aperture: int32 [4096], replicated, may hold values from 640 to 1280
- centroid_table: int32 [64], replicated, may hold values from -160 to 160
- rate_table: float32 [64], replicated, may hold values from 10 to 60
Outputs:
- focused: float32 [2, 2048, 4096], P(None, 'az', 'rg')
All inputs are finite; a program needn't handle non-finite values.
Results may differ from a plain program's by a relative error of at most 0.0003.
Values sent between devices are 32-bit elements; how exact they have to be, the bound alone decides.
A program may use at most 128 MiB of HBM per device.

v0:
```python
from functools import partial
import math

import jax
import jax.numpy as jnp
from jax import lax
from jax.sharding import PartitionSpec as P

chirp_cycles = 300.0
beta_factor = 1.5
shift_gain = 0.2
migration_gain = 0.05


def padded(cells, sides, width):
    for axis, dim in sides:
        count = lax.axis_size(axis)
        ends = count - 1
        head = lax.slice_in_dim(cells, 0, width, axis=dim)
        tail = lax.slice_in_dim(cells, cells.shape[dim] - width, cells.shape[dim], axis=dim)
        cells = jnp.concatenate(
            [
                lax.ppermute(tail, axis, [(i, (i + 1) % count) for i in range(ends)]),
                cells,
                lax.ppermute(head, axis, [((i + 1) % count, i) for i in range(ends)]),
            ],
            axis=dim,
        )
    return cells


def shifted(value, axis, steps):
    count = lax.axis_size(axis)
    leading, last = (max(0, -steps), min(count, count - steps))
    return lax.ppermute(value, axis, [(source, source + steps) for source in range(leading, last)])


def doppler_terms(doppler_bin, centroid, length):
    offset = (doppler_bin - centroid + length // 2) % length - length // 2
    doppler = (centroid + offset).astype(jnp.float32) / length
    migration = jnp.sqrt(1.0 - beta_factor * doppler * doppler)
    scaling = 1.0 / migration - 1.0
    return (offset, migration, scaling)


def phase_one(scaling, range_time):
    lagged = range_time - shift_gain * scaling
    return -math.pi * chirp_cycles * scaling * lagged * lagged


def phase_two(migration, scaling, frequency, total):
    fraction = frequency.astype(jnp.float32) / total
    return math.pi * chirp_cycles * fraction * fraction * migration / (
        1.0 + scaling
    ) + 2.0 * math.pi * migration_gain * scaling * frequency.astype(jnp.float32)


def phase_three(migration, scaling, pulse_rate, range_time):
    return (
        2.0 * math.pi * pulse_rate * (migration - 1.0)
        + math.pi * chirp_cycles * scaling * (1.0 + scaling) * range_time * range_time
    )


def split_pair(total, step, least):
    for candidate in range(step, total + 1, step):
        if total % candidate == 0 and candidate * candidate >= least:
            return (candidate, total // candidate)
    return (total, 1)


def angles(count, row_index, col_index, sign):
    product = row_index[:, None] * col_index[None, :] % count
    return product.astype(jnp.float32) * (sign * 2.0 * math.pi / count)


def rotate(data, angle):
    cosine = jnp.cos(angle)
    sine = jnp.sin(angle)
    return jnp.stack([data[0] * cosine - data[1] * sine, data[0] * sine + data[1] * cosine])


def complex_product(angle, data, form):
    cosine = jnp.cos(angle)
    sine = jnp.sin(angle)
    contract = partial(jnp.einsum, form, precision=lax.Precision.HIGHEST)
    return jnp.stack(
        [
            contract(cosine, data[0]) - contract(sine, data[1]),
            contract(cosine, data[1]) + contract(sine, data[0]),
        ]
    )


def range_forward(data, coarse_size, fine_size):
    total = coarse_size * fine_size
    row_count = data.shape[1]
    coarse_index = jnp.arange(coarse_size, dtype=jnp.int32)
    fine_index = jnp.arange(fine_size, dtype=jnp.int32)
    shaped = data.reshape(2, row_count, coarse_size, fine_size)
    spread = complex_product(
        angles(coarse_size, coarse_index, coarse_index, -1.0), shaped, "kt,mtc->mkc"
    )
    spread = rotate(spread, angles(total, coarse_index, fine_index, -1.0))
    return complex_product(
        angles(fine_size, fine_index, fine_index, -1.0), spread, "jt,mkt->mkj"
    ) * (1.0 / math.sqrt(total))


def range_inverse(spectrum, coarse_size, fine_size):
    total = coarse_size * fine_size
    row_count = spectrum.shape[1]
    coarse_index = jnp.arange(coarse_size, dtype=jnp.int32)
    fine_index = jnp.arange(fine_size, dtype=jnp.int32)
    mixed = complex_product(angles(fine_size, fine_index, fine_index, 1.0), spectrum, "nj,mkj->mkn")
    mixed = rotate(mixed, angles(total, coarse_index, fine_index, 1.0))
    field = complex_product(
        angles(coarse_size, coarse_index, coarse_index, 1.0), mixed, "pk,mkn->mpn"
    ) * (1.0 / math.sqrt(total))
    return field.reshape(2, row_count, total)


def range_work(data, doppler_bins, length, centroid, pulse_rate, aperture, coarse_size, fine_size):
    total = coarse_size * fine_size
    range_bins = jnp.arange(total, dtype=jnp.int32)
    range_time = (range_bins.astype(jnp.float32) + 0.5) / total - 0.5
    offset, migration, scaling = doppler_terms(doppler_bins[:, None], centroid[None, :], length)
    data = rotate(data, phase_one(scaling, range_time[None, :]))
    spectrum = range_forward(data, coarse_size, fine_size)
    coarse_index = jnp.arange(coarse_size, dtype=jnp.int32)
    fine_index = jnp.arange(fine_size, dtype=jnp.int32)
    frequency_bin = fine_index[None, :] * coarse_size + coarse_index[:, None]
    frequency = (frequency_bin + total // 2) % total - total // 2
    unused, migration_zero, scaling_zero = doppler_terms(
        doppler_bins, jnp.zeros_like(doppler_bins), length
    )
    spectrum = rotate(
        spectrum,
        phase_two(
            migration_zero[:, None, None], scaling_zero[:, None, None], frequency[None], total
        ),
    )
    field = range_inverse(spectrum, coarse_size, fine_size)
    field = rotate(field, phase_three(migration, scaling, pulse_rate[None, :], range_time[None, :]))
    keep = 2 * jnp.abs(offset) < aperture[None, :]
    return jnp.where(keep[None], field, 0.0)


def per_device(echo, range_row, aperture, centroid_table, rate_table):
    segment = echo.shape[1]
    range_width = echo.shape[2]
    length = 5 * segment
    groups = lax.axis_size("rg")
    position = lax.axis_index("rg")
    range_total = range_width * groups
    outer_size, inner_size = split_pair(length, groups, length)
    fine_range, coarse_range = split_pair(range_total, 1, 4 * range_total)
    scale_az = 1.0 / math.sqrt(length)
    near = padded(echo, (("az", 1),), segment)
    before = shifted(echo, "az", 2)
    after = shifted(echo, "az", -2)
    block = jnp.concatenate([before, near, after], axis=1)
    table_index = jnp.arange(centroid_table.shape[0], dtype=jnp.int32)
    onehot = range_row[:, None] == table_index[None, :]
    centroid = jnp.sum(jnp.where(onehot, centroid_table[None, :], 0), axis=1)
    pulse_rate = jnp.sum(jnp.where(onehot, rate_table[None, :], 0.0), axis=1)
    outer_index = jnp.arange(outer_size, dtype=jnp.int32)
    inner_index = jnp.arange(inner_size, dtype=jnp.int32)
    shaped = block.reshape(2, outer_size, inner_size, range_width)
    spread = complex_product(
        angles(outer_size, outer_index, outer_index, -1.0), shaped, "kt,tar->kar"
    )
    spread = rotate(spread, angles(length, outer_index, inner_index, -1.0)[:, :, None])
    spectrum = (
        complex_product(angles(inner_size, inner_index, inner_index, -1.0), spread, "jt,ktr->jkr")
        * scale_az
    )
    spectrum = spectrum.reshape(2, length, range_width)
    turned = lax.all_to_all(spectrum, "rg", split_axis=1, concat_axis=2, tiled=True)
    row_count = turned.shape[1]
    doppler_bins = position * row_count + jnp.arange(row_count, dtype=jnp.int32)
    worked = range_work(
        turned, doppler_bins, length, centroid, pulse_rate, aperture, coarse_range, fine_range
    )
    returned = lax.all_to_all(worked, "rg", split_axis=2, concat_axis=1, tiled=True)
    returned = returned.reshape(2, inner_size, outer_size, range_width)
    mixed = complex_product(
        angles(inner_size, inner_index, inner_index, 1.0), returned, "nj,jqr->nqr"
    )
    mixed = rotate(mixed, angles(length, inner_index, outer_index, 1.0)[:, :, None])
    field = (
        complex_product(angles(outer_size, outer_index, outer_index, 1.0), mixed, "pq,nqr->pnr")
        * scale_az
    )
    field = field.reshape(2, length, range_width)
    return field[:, 2 * segment : 3 * segment]


def solution(mesh):
    in_specs = (P(None, "az", "rg"), P(), P(), P(), P())
    out_specs = P(None, "az", "rg")
    return jax.shard_map(
        per_device, mesh=mesh, in_specs=in_specs, out_specs=out_specs, check_vma=False
    )
```

profile of v0, /device:TPU:27, one launch (start us, length us, event | category | flops | bytes accessed | tf_op | source)
XLA Modules:
  0.0 290.4 jit_solution(9481324489207708223)
XLA Ops:
  0.0 3.7 %collective-permute-start = (f32[2,256,256]{2,1,0:T(8,128)}, f32[2,256,256]{2,1,0:T(8,128)S(1)}, u32[]{:S(2)}, u32[]{:S(2)}) collective-permute-start(f32[2,256,256]{2,1,0:T(8,128)} %param.5), channel_id=1, source_target_pairs={{0,32},{16,48},{32,64},{48,80},{64,96},{80,112},{1,33},{17,49},{33... | collective-permute-start | bytes 1572872 | tf_op jit(solution)/shard_map/ppermute | solution.py:35
  3.7 3.5 %collective-permute-start.1 = (f32[2,256,256]{2,1,0:T(8,128)}, f32[2,256,256]{2,1,0:T(8,128)S(1)}, u32[]{:S(2)}, u32[]{:S(2)}) collective-permute-start(f32[2,256,256]{2,1,0:T(8,128)} %param.5), channel_id=1, source_target_pairs={{0,16},{16,32},{32,48},{48,64},{64,80},{80,96},{96,112},{1,17},{17... | collective-permute-start | bytes 1572872 | tf_op jit(solution)/shard_map/ppermute | solution.py:23
  7.2 1.9 collective-permute-start.2
  10.5 4.0 %collective-permute-done = f32[2,256,256]{2,1,0:T(8,128)S(1)} collective-permute-done((f32[2,256,256]{2,1,0:T(8,128)}, f32[2,256,256]{2,1,0:T(8,128)S(1)}, u32[]{:S(2)}, u32[]{:S(2)}) %collective-permute-start) | collective-permute-done | bytes 524320 | tf_op jit(solution)/shard_map/ppermute | solution.py:35
  14.6 3.7 %collective-permute-done.1 = f32[2,256,256]{2,1,0:T(8,128)S(1)} collective-permute-done((f32[2,256,256]{2,1,0:T(8,128)}, f32[2,256,256]{2,1,0:T(8,128)S(1)}, u32[]{:S(2)}, u32[]{:S(2)}) %collective-permute-start.1) | collective-permute-done | bytes 524320 | tf_op jit(solution)/shard_map/ppermute | solution.py:23
  18.4 12.5 %collective-permute-done.2 = f32[2,256,256]{2,1,0:T(8,128)S(1)} collective-permute-done((f32[2,256,256]{2,1,0:T(8,128)}, f32[2,256,256]{2,1,0:T(8,128)S(1)}, u32[]{:S(2)}, u32[]{:S(2)}) %collective-permute-start.2) | collective-permute-done | bytes 524320 | tf_op jit(solution)/shard_map/ppermute | solution.py:25
  30.9 3.6 %collective-permute-done.3 = f32[2,256,256]{2,1,0:T(8,128)S(1)} collective-permute-done((f32[2,256,256]{2,1,0:T(8,128)}, f32[2,256,256]{2,1,0:T(8,128)S(1)}, u32[]{:S(2)}, u32[]{:S(2)}) %collective-permute-start.3) | collective-permute-done | bytes 524320 | tf_op jit(solution)/shard_map/ppermute | solution.py:35
  35.9 2.7 fusion.60
  38.7 1.7 squeeze.20
  40.4 1.7 fusion.62
  42.0 1.7 convolution_subtract_fusion.3
  43.7 2.1 multiply_subtract_fusion.6
  45.9 2.1 fusion.10
  47.9 2.1 fusion.8
  50.0 2.1 fusion.16
  53.1 2.1 fusion.19
  55.8 8.4 %copy.132 = f32[2,1280,256]{2,0,1:T(2,128)} copy(f32[2,1280,256]{2,1,0:T(8,128)S(1)} %maximum_multiply_fusion) | data formatting | bytes 5242880 | tf_op jit(solution)/shard_map/mul | solution.py:175
  64.3 8.9 %all-to-all-start = ((f32[2,1280,256]{2,0,1:T(2,128)}), f32[2,1280,256]{2,0,1:T(2,128)S(1)}, u32[]{:S(2)}, u32[]{:S(2)}) async-start(f32[2,1280,256]{2,0,1:T(2,128)} %copy.132), calls=%async_computation | async-start | bytes 5242880 | tf_op jit(solution)/shard_map/all_to_all | solution.py:179
  75.2 36.8 %all-to-all-done = f32[2,1280,256]{2,0,1:T(2,128)S(1)} async-done(((f32[2,1280,256]{2,0,1:T(2,128)}), f32[2,1280,256]{2,0,1:T(2,128)S(1)}, u32[]{:S(2)}, u32[]{:S(2)}) %all-to-all-start) | async-done | bytes 2621472 | tf_op jit(solution)/shard_map/all_to_all | solution.py:179
  112.0 3.1 %fusion.365 = (f32[1,80,16,256]{3,0,1,2:T(1,128)S(1)}, f32[1,80,16,256]{3,0,1,2:T(1,128)}) fusion(f32[2,80,16,256]{3,0,1,2:T(2,128)S(1)} %bitcast.138), kind=kLoop, calls=%fused_computation.413 | loop fusion | bytes 5242880 | tf_op jit(solution)/shard_map/slice | solution.py:80
  120.2 9.1 %fusion.142 = f32[80,128,32]{1,2,0:T(8,128)S(1)} fusion(f32[80,32,128]{2,1,0:T(8,128)} %squeeze.23, f32[80,32,128]{2,1,0:T(8,128)S(1)} %copy-done.4, f32[32,128]{1,0:T(8,128)S(1)} %multiply_add_fusion.14, s32[80]{0:T(128)S(1)} %iota_add_fusion, s32[32,128]{1,0:T(8,128)S(1)} %bitcast.142), kind=kOutput, calls=%fused_computation.198 | convolution fusion | flops 133707776 | bytes 3965248 | tf_op jit(solution)/shard_map/kt,mtc->mkc/dot_general | solution.py:89
  129.2 7.3 %fusion.140 = f32[80,128,32]{1,2,0:T(8,128)S(1)} fusion(f32[80,32,128]{2,1,0:T(8,128)S(1)} %copy-done.5, f32[80,32,128]{2,1,0:T(8,128)S(1)} %copy-done.4, f32[32,128]{1,0:T(8,128)S(1)} %multiply_add_fusion.14, s32[80]{0:T(128)S(1)} %iota_add_fusion, s32[32,128]{1,0:T(8,128)S(1)} %bitcast.143), kind=kOutput, calls=%fused_computation.196 | convolution fusion | flops 133707776 | bytes 3965248 | tf_op jit(solution)/shard_map/kt,mtc->mkc/dot_general | solution.py:90
  136.5 7.8 %fusion.33 = f32[80,32,128]{2,1,0:T(8,128)S(1)} fusion(f32[80,128,32]{1,2,0:T(8,128)S(1)} %fusion.142, f32[80,32,128]{2,1,0:T(8,128)S(1)} %copy-done.5, f32[80,32,128]{2,1,0:T(8,128)S(1)} %copy-done.4, f32[32,128]{1,0:T(8,128)S(1)} %multiply_add_fusion.14, s32[80]{0:T(128)S(1)} %iota_add_fusion, s32[32,128]{1,0:T(8,128)S(1)} %bitcast.144), kind=kOutput, calls=%fused_computation.47 | convolution fusion | flops 134035456 | bytes 5275968 | tf_op jit(solution)/shard_map/kt,mtc->mkc/dot_general | solution.py:89
  144.4 7.4 %fusion.32 = f32[80,32,128]{2,1,0:T(8,128)S(1)} fusion(f32[80,128,32]{1,2,0:T(8,128)S(1)} %fusion.140, f32[80,32,128]{2,1,0:T(8,128)S(1)} %copy-done.5, f32[80,32,128]{2,1,0:T(8,128)S(1)} %copy-done.4, f32[32,128]{1,0:T(8,128)S(1)} %multiply_add_fusion.14, s32[80]{0:T(128)S(1)} %iota_add_fusion, s32[32,128]{1,0:T(8,128)S(1)} %bitcast.145), kind=kOutput, calls=%fused_computation.45 | convolution fusion | flops 134035456 | bytes 5275968 | tf_op jit(solution)/shard_map/kt,mtc->mkc/dot_general | solution.py:90
  151.8 2.5 fusion.72
  154.3 1.5 fusion.73
  155.8 1.5 fusion.28
  157.3 1.5 fusion.29
  159.1 5.7 %multiply_subtract_fusion.3 = (f32[80,32,128]{2,1,0:T(8,128)S(1)}, f32[80,32,128]{2,1,0:T(8,128)S(1)}) fusion(f32[2,80,32,128]{3,2,1,0:T(8,128)S(1)} %maximum_multiply_fusion.1, f32[32,128]{1,0:T(8,128)S(1)} %fusion.133, f32[80]{0:T(128)S(1)} %get-tuple-element.23, f32[80]{0:T(128)S(1)} %get-tuple-element.24, f32[80]{0:T(128)S(1)} %fusion.362, ...), kind=kLoop, calls=%fused_computation.69 | loop fusion | flops 3276800 | bytes 5276608 | tf_op jit(solution)/shard_map/sub | solution.py:80
  164.8 1.5 fusion.82
  167.7 1.5 convolution_subtract_fusion.1
  169.2 1.5 convolution_add_fusion.1
  173.6 1.5 fusion.31
  175.1 1.5 fusion.30
  180.5 7.8 %multiply_subtract_fusion.1 = (f32[1,80,4096]{2,1,0:T(8,128)S(1)}, f32[1,80,4096]{2,1,0:T(8,128)S(1)}) fusion(f32[1,80,4096]{2,1,0:T(8,128)} %squeeze.51, f32[1,80,4096]{2,1,0:T(8,128)S(1)} %copy-done.2, f32[4096]{0:T(1024)S(1)} %get-tuple-element.29, s32[80]{0:T(128)S(1)} %iota_add_fusion, s32[4096]{0:T(1024)S(1)} %select_reduce_fusion.1, ...), kind=kLoop, calls=%fused_computation.61 | loop fusion | flops 9830400 | bytes 5292352 | tf_op jit(solution)/shard_map/sub | solution.py:80
  188.6 4.4 %copy.135 = f32[2,80,4096]{1,0,2:T(2,128)} copy(f32[2,80,4096]{2,1,0:T(8,128)S(1)} %maximum_select_fusion) | data formatting | bytes 5242880 | tf_op jit(solution)/shard_map/jit(_where)/select_n | solution.py:146
  193.1 4.4 %all-to-all-start.1 = ((f32[2,80,4096]{1,0,2:T(2,128)}), f32[2,80,4096]{1,0,2:T(2,128)}, u32[]{:S(2)}, u32[]{:S(2)}) async-start(f32[2,80,4096]{1,0,2:T(2,128)} %copy.135), calls=%async_computation.1 | async-start | bytes 8388608 | tf_op jit(solution)/shard_map/all_to_all | solution.py:185
  197.7 62.5 %all-to-all-done.1 = f32[2,80,4096]{1,0,2:T(2,128)} async-done(((f32[2,80,4096]{1,0,2:T(2,128)}), f32[2,80,4096]{1,0,2:T(2,128)}, u32[]{:S(2)}, u32[]{:S(2)}) %all-to-all-start.1) | async-done | bytes 2621472 | tf_op jit(solution)/shard_map/all_to_all | solution.py:185
  260.2 3.8 %copy.149 = f32[2,80,16,256]{3,2,1,0:T(8,128)S(1)} copy(f32[2,80,16,256]{1,0,3,2:T(2,128)} %bitcast.30) | data formatting | bytes 5242880 | tf_op jit(solution)/shard_map/all_to_all | solution.py:185
  265.0 2.1 fusion.2
  267.0 2.1 fusion
  269.9 2.1 fusion.22
  272.0 2.6 multiply_subtract_fusion
  274.6 1.8 fusion.57
  276.5 2.7 fusion.53
  279.2 1.7 convolution_subtract_fusion
  282.8 3.0 %convolution_add_fusion = f32[64,20,256]{2,0,1:T(8,128)S(1)} fusion(f32[64,20,256]{2,0,1:T(8,128)} %fusion.53, f32[20,64,256]{2,0,1:T(8,128)S(1)} %get-tuple-element.5), kind=kOutput, calls=%fused_computation.30 | convolution fusion | flops 252043264 | bytes 3932160 | tf_op jit(solution)/shard_map/pq,nqr->pnr/dot_general | solution.py:90
  288.4 1.8 fusion.71
  (68 shorter events, 26.9 us)
Async XLA Ops:
  0.0 18.3 %copy-start.6 = (f32[2,256,256]{2,1,0:T(8,128)S(1)}, f32[2,256,256]{2,1,0:T(8,128)}, u32[]{:S(2)}) copy-start(f32[2,256,256]{2,1,0:T(8,128)} %param.5) | copy-start | bytes 1572868
  0.0 14.6 %collective-permute-start = (f32[2,256,256]{2,1,0:T(8,128)}, f32[2,256,256]{2,1,0:T(8,128)S(1)}, u32[]{:S(2)}, u32[]{:S(2)}) collective-permute-start(f32[2,256,256]{2,1,0:T(8,128)} %param.5), channel_id=1, source_target_pairs={{0,32},{16,48},{32,64},{48,80},{64,96},{80,112},{1,33},{17,49},{33... | collective-permute-start | bytes 1572872 | tf_op jit(solution)/shard_map/ppermute | solution.py:35
  3.7 14.6 %collective-permute-start.1 = (f32[2,256,256]{2,1,0:T(8,128)}, f32[2,256,256]{2,1,0:T(8,128)S(1)}, u32[]{:S(2)}, u32[]{:S(2)}) collective-permute-start(f32[2,256,256]{2,1,0:T(8,128)} %param.5), channel_id=1, source_target_pairs={{0,16},{16,32},{32,48},{48,64},{64,80},{80,96},{96,112},{1,17},{17... | collective-permute-start | bytes 1572872 | tf_op jit(solution)/shard_map/ppermute | solution.py:23
  7.2 23.7 %collective-permute-start.2 = (f32[2,256,256]{2,1,0:T(8,128)}, f32[2,256,256]{2,1,0:T(8,128)S(1)}, u32[]{:S(2)}, u32[]{:S(2)}) collective-permute-start(f32[2,256,256]{2,1,0:T(8,128)} %param.5), channel_id=1, source_target_pairs={{16,0},{32,16},{48,32},{64,48},{80,64},{96,80},{112,96},{17,1},{33... | collective-permute-start | bytes 1572872 | tf_op jit(solution)/shard_map/ppermute | solution.py:25
  9.1 25.4 %collective-permute-start.3 = (f32[2,256,256]{2,1,0:T(8,128)}, f32[2,256,256]{2,1,0:T(8,128)S(1)}, u32[]{:S(2)}, u32[]{:S(2)}) collective-permute-start(f32[2,256,256]{2,1,0:T(8,128)} %param.5), channel_id=1, source_target_pairs={{32,0},{48,16},{64,32},{80,48},{96,64},{112,80},{33,1},{49,17},{65... | collective-permute-start | bytes 1572872 | tf_op jit(solution)/shard_map/ppermute | solution.py:35
  40.3 1.7 copy-start.3
  64.3 9.1 %copy-start.7 = (s32[4096]{0:T(1024)S(1)}, s32[4096]{0:T(1024)}, u32[]{:S(2)}) copy-start(s32[4096]{0:T(1024)} %param.6) | copy-start | bytes 49156
  64.3 9.2 %copy-start.9 = (s32[64]{0:T(128)S(1)}, s32[64]{0:T(128)}, u32[]{:S(2)}) copy-start(s32[64]{0:T(128)} %param.8) | copy-start | bytes 772
  64.3 9.4 %copy-start.10 = (f32[64]{0:T(128)S(1)}, f32[64]{0:T(128)}, u32[]{:S(2)}) copy-start(f32[64]{0:T(128)} %param.9) | copy-start | bytes 772
  64.3 9.7 %copy-start.8 = (s32[4096]{0:T(1024)S(1)}, s32[4096]{0:T(1024)}, u32[]{:S(2)}) copy-start(s32[4096]{0:T(1024)} %param.7) | copy-start | bytes 49156
  64.3 47.7 %all-to-all-start = ((f32[2,1280,256]{2,0,1:T(2,128)}), f32[2,1280,256]{2,0,1:T(2,128)S(1)}, u32[]{:S(2)}, u32[]{:S(2)}) async-start(f32[2,1280,256]{2,0,1:T(2,128)} %copy.132), calls=%async_computation | async-start | bytes 5242880 | tf_op jit(solution)/shard_map/all_to_all | solution.py:179
  115.8 1.8 copy-start
  118.4 1.8 copy-start.4
  120.1 9.1 %copy-start.5 = (f32[80,32,128]{2,1,0:T(8,128)S(1)}, f32[80,32,128]{2,1,0:T(8,128)}, u32[]{:S(2)}) copy-start(f32[80,32,128]{2,1,0:T(8,128)} %squeeze.23) | copy-start | bytes 3932164
  178.8 1.7 copy-start.2
  193.1 67.1 %all-to-all-start.1 = ((f32[2,80,4096]{1,0,2:T(2,128)}), f32[2,80,4096]{1,0,2:T(2,128)}, u32[]{:S(2)}, u32[]{:S(2)}) async-start(f32[2,80,4096]{1,0,2:T(2,128)} %copy.135), calls=%async_computation.1 | async-start | bytes 8388608 | tf_op jit(solution)/shard_map/all_to_all | solution.py:185
  286.6 1.8 copy-start.1
where the time goes:
time: 294 us; the launch traced here: 290 us
  waiting for transfers between devices  123 us (42%)
  matrix products  84.8 us (29%)
  local copies, waits for them, and re-layouts  38.9 us (13%)
  starting transfers between devices  23.7 us (8%)
  other arithmetic  19 us (6%)
    all_to_all x1, waiting for transfers between devices, per_device(): lax.all_to_all(worked, 'rg', split_axis=2, concat_axis=1, tiled=True)  62.5 us
    all_to_all x1, waiting for transfers between devices, per_device(): lax.all_to_all(spectrum, 'rg', split_axis=1, concat_axis=2, tiled=True)  36.8 us
    dot_general x8, matrix products, complex_product(): contract(cosine, data[0]) - contract(sine, data[1])  22.2 us
    dot_general x8, matrix products, complex_product(): contract(sine, data[0])  21.1 us
    dot_general x8, matrix products, complex_product(): contract(sine, data[1])  20.8 us
    dot_general x8, matrix products, complex_product(): contract(cosine, data[1]) + contract(sine, data[0])  20.7 us
    sub x2, other arithmetic, rotate(): data[0] * cosine - data[1] * sine  13.5 us
    ppermute x1, waiting for transfers between devices, padded(): lax.ppermute(head, axis, [((i + 1) % count, i) for i in range(ends)])  12.5 us
  transfers between devices with their start and end apart: 6, of which 6 were waited for; matrix products, arithmetic and copies ran while one was open for 1% of the time, Pallas kernels for 0%

commit v1 on v0

v1 whole, which is shorter than its diff:
```python
from functools import partial
import math

import jax
import jax.numpy as jnp
import numpy as np
from jax import lax
from jax.experimental import pallas as pl
from jax.experimental.pallas import tpu as pltpu
from jax.sharding import PartitionSpec as P
import ml_dtypes

F32 = jnp.float32
BF16 = jnp.bfloat16
MESH = pl.DeviceIdType.MESH

SEG = 256
CLASSES = 5
LENGTH = SEG * CLASSES
GROUPS = 16
WIDTH = 256
TOTAL = GROUPS * WIDTH
LINES = SEG // GROUPS
HALF = 128
OTHERS = GROUPS - 1

STEPS = [
    (dx, dy, dc)
    for dc in (0, 1)
    for dx, dy in ((1, 2), (0, 2), (1, 1), (1, 3), (0, 1), (0, 3), (1, 0), (0, 0))
    if (dx, dy, dc) != (0, 0, 0)
]


def pair_split(values):
    high = values.astype(ml_dtypes.bfloat16)
    low = (values - high.astype(np.float64)).astype(ml_dtypes.bfloat16)
    return np.stack([high, low])


def azimuth_tables():
    p = np.arange(SEG)[None, :, None]
    m = np.arange(SEG)[None, None, :]
    q = np.arange(CLASSES)[:, None, None]
    turns = ((2 * SEG + p) * (CLASSES * m + q)) % LENGTH
    angle = turns * (2.0 * np.pi / LENGTH)
    scale = 1.0 / math.sqrt(LENGTH)
    cosine, sine = np.cos(angle) * scale, np.sin(angle) * scale
    inverse = np.concatenate([cosine, sine], axis=2)
    forward = np.concatenate([cosine.transpose(0, 2, 1), sine.transpose(0, 2, 1)], axis=2)
    return pair_split(forward).transpose(1, 0, 2, 3), pair_split(inverse).transpose(1, 0, 2, 3)


def range_tables():
    index = np.arange(WIDTH)
    angle = (index[:, None] * index[None, :] % WIDTH) * (2.0 * np.pi / WIDTH)
    cosine, sine = np.cos(angle), np.sin(angle)
    forward = np.block([[cosine, -sine], [sine, cosine]])
    inverse = np.block([[cosine, sine], [-sine, cosine]])
    fine = np.arange(GROUPS)[:, None] * index[None, :] * (2.0 * np.pi / TOTAL)
    twiddle = np.stack([np.cos(fine), np.sin(fine)]).astype(np.float32)
    return np.stack([pair_split(forward), pair_split(inverse)]), twiddle


def segment_weights():
    q = np.arange(CLASSES)[:, None]
    step = np.arange(1, 3)[None, :]
    angle = (q * step % CLASSES) * (2.0 * np.pi / CLASSES)
    return np.concatenate([np.cos(angle), np.sin(angle)], axis=1).astype(np.float32)


def split(value):
    high = value.astype(BF16)
    return high, (value - high.astype(F32)).astype(BF16)


def fitted(function, powers):
    nodes = np.cos((np.arange(400) + 0.5) * np.pi / 400) * 0.5
    nodes = nodes[nodes > 0]
    basis = np.stack([(2 * nodes) ** p for p in powers], axis=1)
    solved = np.linalg.lstsq(basis, function(2.0 * np.pi * nodes), rcond=None)[0]
    return [float(value * 2.0**p) for value, p in zip(solved, powers)]


SINE = fitted(np.sin, [1, 3, 5, 7, 9, 11])
COSINE = fitted(np.cos, [0, 2, 4, 6, 8, 10, 12])


def turn(cycles):
    left = cycles - jnp.floor(cycles + 0.5)
    square = left * left
    sine, cosine = SINE[-1], COSINE[-1]
    for value in SINE[-2::-1]:
        sine = sine * square + value
    for value in COSINE[-2::-1]:
        cosine = cosine * square + value
    return cosine, sine * left


def times_turn(value, quarter):
    real, imag = value
    quarter %= 4
    if quarter == 0:
        return real, imag
    if quarter == 1:
        return -imag, real
    if quarter == 2:
        return -real, -imag
    return imag, -real


def four(values, sign):
    a, b, c, d = values
    ac = (a[0] + c[0], a[1] + c[1])
    am = (a[0] - c[0], a[1] - c[1])
    bd = (b[0] + d[0], b[1] + d[1])
    bm = times_turn((b[0] - d[0], b[1] - d[1]), sign)
    return [
        (ac[0] + bd[0], ac[1] + bd[1]),
        (am[0] + bm[0], am[1] + bm[1]),
        (ac[0] - bd[0], ac[1] - bd[1]),
        (am[0] - bm[0], am[1] - bm[1]),
    ]


def sixteen(values, sign):
    inner = [four(values[low::4], sign) for low in range(4)]
    result = [None] * 16
    for first in range(4):
        column = []
        for low in range(4):
            real, imag = inner[low][first]
            step = low * first
            if step % 4 == 0:
                column.append(times_turn((real, imag), sign * (step // 4)))
            else:
                angle = sign * 2.0 * math.pi * step / 16
                cosine, sine = math.cos(angle), math.sin(angle)
                if step % 2 == 0:
                    root = math.sqrt(0.5)
                    up = 1.0 if cosine > 0 else -1.0
                    side = 1.0 if sine > 0 else -1.0
                    if up == side:
                        column.append(((real - imag) * (up * root), (real + imag) * (up * root)))
                    else:
                        column.append(((real + imag) * (up * root), (imag - real) * (up * root)))
                else:
                    column.append((real * cosine - imag * sine, real * sine + imag * cosine))
        outer = four(column, sign)
        for second in range(4):
            result[first + 4 * second] = outer[second]
    return result


def dot(left, right):
    return jnp.dot(left, right, preferred_element_type=F32)


def kernel(
    echo,
    range_row,
    aperture,
    twiddle,
    centroid_table,
    rate_table,
    weights,
    forward_hbm,
    inverse_hbm,
    range_hbm,
    out,
    forward,
    inverse,
    dense,
    halo,
    sums,
    made,
    got,
    back,
    home,
    one,
    two,
    three,
    centroid,
    rate,
    left,
    mixed,
    total,
    const_sem,
    halo_send,
    halo_recv,
    made_send,
    made_recv,
    back_send,
    back_recv,
):
    az = lax.axis_index("az")
    me = lax.axis_index("rg")
    high, middle, core = me // 8, (me // 2) % 4, me % 2
    partners = [
        ((high + dx) % 2) * 8 + ((middle + dy) % 4) * 2 + (core + dc) % 2 for dx, dy, dc in STEPS
    ]
    around = [(az + step) % 8 for step in (2, 6, 1, 7)]

    barrier = pltpu.get_barrier_semaphore()
    for other in around:
        pl.semaphore_signal(barrier, inc=1, device_id=(other, me), device_id_type=MESH)
    for partner in partners:
        pl.semaphore_signal(barrier, inc=1, device_id=(az, partner), device_id_type=MESH)
    consts = [
        pltpu.make_async_copy(range_hbm, dense, const_sem.at[0]),
        pltpu.make_async_copy(forward_hbm, forward, const_sem.at[1]),
        pltpu.make_async_copy(inverse_hbm, inverse, const_sem.at[2]),
    ]
    for copy in consts:
        copy.start()
    pl.semaphore_wait(barrier, len(around) + OTHERS)

    halo_copies = []
    for side in range(2):
        columns = pl.ds(side * HALF, HALF)
        for slot, other in enumerate(around):
            copy = pltpu.make_async_remote_copy(
                src_ref=echo.at[:, :, columns],
                dst_ref=halo.at[side, slot],
                send_sem=halo_send.at[side, slot],
                recv_sem=halo_recv.at[side, slot],
                device_id=(other, me),
                device_id_type=MESH,
            )
            copy.start()
            halo_copies.append(copy)

    rows = range_row[...]
    centers = jnp.zeros((GROUPS, WIDTH), jnp.int32)
    rates = jnp.zeros((GROUPS, WIDTH), F32)
    for entry in range(64):
        hit = rows == entry
        centers = jnp.where(hit, centroid_table[entry], centers)
        rates = jnp.where(hit, rate_table[entry], rates)
    centroid[...] = centers
    rate[...] = rates

    lane = lax.broadcasted_iota(jnp.int32, (LINES, WIDTH), 1)
    line = lax.broadcasted_iota(jnp.int32, (LINES, WIDTH), 0)

    def doppler(bins):
        fraction = bins.astype(F32) * (1.0 / LENGTH)
        squared = jnp.maximum(1.0 - 1.5 * fraction * fraction, 0.1)
        migration = jnp.sqrt(squared)
        return squared, migration, 1.0 / migration - 1.0

    def phases(q, carry):
        bins = CLASSES * (LINES * me + line) + q
        unused, low_migration, low_scaling = doppler(bins)
        unused, high_migration, high_scaling = doppler(bins - LENGTH)
        squared, unused, zero_scaling = doppler(jnp.where(bins < LENGTH // 2, bins, bins - LENGTH))
        square_gain = squared * (150.0 / (TOTAL * TOTAL))
        linear_gain = zero_scaling * 0.05

        def each_group(g, inner):
            here = pl.ds(g, 1)
            center = centroid[here, :]
            time = (g * WIDTH + lane).astype(F32) * (1.0 / TOTAL) + (0.5 / TOTAL - 0.5)
            low = bins <= center + (LENGTH // 2 - 1)
            migration = jnp.where(low, low_migration, high_migration)
            scaling = jnp.where(low, low_scaling, high_scaling)
            offset = jnp.where(low, bins, bins - LENGTH) - center
            lagged = time - 0.2 * scaling
            cosine, sine = turn(-150.0 * scaling * lagged * lagged)
            one[0, q, g] = cosine
            one[1, q, g] = sine
            cosine, sine = turn(
                rate[here, :] * (migration - 1.0) + 150.0 * scaling * (1.0 + scaling) * time * time
            )
            keep = jnp.where(2 * jnp.abs(offset) < aperture[here, :], 1.0 / TOTAL, 0.0)
            three[0, q, g] = cosine * keep
            three[1, q, g] = sine * keep
            frequency = (GROUPS * lane + g - jnp.where(lane >= HALF, TOTAL, 0)).astype(F32)
            cosine, sine = turn((square_gain * frequency + linear_gain) * frequency)
            two[0, q, g] = cosine
            two[1, q, g] = sine
            return inner

        return lax.fori_loop(0, GROUPS, each_group, carry)

    lax.fori_loop(0, CLASSES, phases, 0)

    consts[1].wait()
    valid = [
        jnp.where(az >= 2, 1.0, 0.0).astype(F32),
        jnp.where(az < 6, 1.0, 0.0).astype(F32),
        jnp.where(az >= 1, 1.0, 0.0).astype(F32),
        jnp.where(az < 7, 1.0, 0.0).astype(F32),
    ]
    mine = pl.ds(pl.multiple_of(me * LINES, LINES), LINES)
    for side in range(2):
        for slot in range(4):
            halo_copies[side * 4 + slot].wait_recv()
        for part in range(2):
            before_two = halo[side, 0, part] * valid[0]
            after_two = halo[side, 1, part] * valid[1]
            before_one = halo[side, 2, part] * valid[2]
            after_one = halo[side, 3, part] * valid[3]
            sums[0, part] = after_one + before_one
            sums[1, part] = after_two + before_two
            sums[2, part] = after_one - before_one
            sums[3, part] = after_two - before_two

        def azimuth(q, carry):
            c_one, c_two, s_one, s_two = (weights[q, i] for i in range(4))
            real = (
                echo[0, :, side * HALF : (side + 1) * HALF]
                + c_one * sums[0, 0]
                + c_two * sums[1, 0]
                + (s_one * sums[2, 1] + s_two * sums[3, 1])
            )
            imag = (
                echo[1, :, side * HALF : (side + 1) * HALF]
                + c_one * sums[0, 1]
                + c_two * sums[1, 1]
                - (s_one * sums[2, 0] + s_two * sums[3, 0])
            )
            real_high, real_low = split(real)
            imag_high, imag_low = split(imag)
            block_high = jnp.concatenate(
                [
                    jnp.concatenate([real_high, imag_high], axis=1),
                    jnp.concatenate([imag_high, -real_high], axis=1),
                ],
                axis=0,
            )
            block_low = jnp.concatenate(
                [
                    jnp.concatenate([real_low, imag_low], axis=1),
                    jnp.concatenate([imag_low, -real_low], axis=1),
                ],
                axis=0,
            )
            spectrum = (
                dot(forward[q, 0], block_high)
                + dot(forward[q, 1], block_high)
                + dot(forward[q, 0], block_low)
            )
            made[q, side, 0] = spectrum[:, :HALF]
            made[q, side, 1] = spectrum[:, HALF:]
            for partner in partners:
                theirs = pl.ds(pl.multiple_of(partner * LINES, LINES), LINES)
                pltpu.make_async_remote_copy(
                    src_ref=made.at[q, side, :, theirs, :],
                    dst_ref=got.at[q, side, me],
                    send_sem=made_send.at[q, side],
                    recv_sem=made_recv.at[q, side],
                    device_id=(az, partner),
                    device_id_type=MESH,
                ).start()
            got[q, side, me] = made[q, side, :, mine, :]
            return carry

        lax.fori_loop(0, CLASSES, azimuth, 0)

    consts[0].wait()

    def range_work(q, carry):
        for side in range(2):
            lot = got.at[q, side, pl.ds(0, OTHERS)]
            pltpu.make_async_copy(lot, lot, made_recv.at[q, side]).wait()
        for upper in range(2):
            some = slice(upper * 8, upper * 8 + 8)
            for side in range(2):
                columns = slice(side * HALF, (side + 1) * HALF)
                values = []
                for g in range(GROUPS):
                    real, imag = got[q, side, g, 0, some, :], got[q, side, g, 1, some, :]
                    cosine, sine = one[0, q, g, some, columns], one[1, q, g, some, columns]
                    values.append((real * cosine - imag * sine, real * sine + imag * cosine))
                values = sixteen(values, -1)
                for g in range(GROUPS):
                    real, imag = values[g]
                    cosine, sine = twiddle[0, g : g + 1, columns], twiddle[1, g : g + 1, columns]
                    values[g] = (real * cosine + imag * sine, imag * cosine - real * sine)
                for g in range(0, GROUPS, 2):
                    place = slice(upper * HALF + g * 8, upper * HALF + g * 8 + 16)
                    for part in range(2):
                        both = jnp.concatenate([values[g][part], values[g + 1][part]], axis=0)
                        spot = slice(part * WIDTH + side * HALF, part * WIDTH + (side + 1) * HALF)
                        left[0, place, spot], left[1, place, spot] = split(both)
        for upper in range(2):
            area = slice(upper * HALF, (upper + 1) * HALF)
            mixed[area, :] = (
                dot(left[0, area, :], dense[0, 0])
                + dot(left[0, area, :], dense[0, 1])
                + dot(left[1, area, :], dense[0, 0])
            )
        for upper in range(2):
            some = slice(upper * 8, upper * 8 + 8)
            for g in range(0, GROUPS, 2):
                place = slice(upper * HALF + g * 8, upper * HALF + g * 8 + 16)
                real, imag = mixed[place, :WIDTH], mixed[place, WIDTH:]
                cosine = jnp.concatenate([two[0, q, g, some, :], two[0, q, g + 1, some, :]], axis=0)
                sine = jnp.concatenate([two[1, q, g, some, :], two[1, q, g + 1, some, :]], axis=0)
                left[0, place, :WIDTH], left[1, place, :WIDTH] = split(real * cosine - imag * sine)
                left[0, place, WIDTH:], left[1, place, WIDTH:] = split(real * sine + imag * cosine)
        for upper in range(2):
            area = slice(upper * HALF, (upper + 1) * HALF)
            mixed[area, :] = (
                dot(left[0, area, :], dense[1, 0])
                + dot(left[0, area, :], dense[1, 1])
                + dot(left[1, area, :], dense[1, 0])
            )
        for upper in range(2):
            some = slice(upper * 8, upper * 8 + 8)
            for side in range(2):
                columns = slice(side * HALF, (side + 1) * HALF)
                values = []
                for g in range(GROUPS):
                    place = slice(upper * HALF + g * 8, upper * HALF + g * 8 + 8)
                    real = mixed[place, side * HALF : (side + 1) * HALF]
                    imag = mixed[place, WIDTH + side * HALF : WIDTH + (side + 1) * HALF]
                    cosine, sine = twiddle[0, g : g + 1, columns], twiddle[1, g : g + 1, columns]
                    values.append((real * cosine - imag * sine, real * sine + imag * cosine))
                values = sixteen(values, 1)
                for g in range(GROUPS):
                    real, imag = values[g]
                    cosine, sine = three[0, q, g, some, columns], three[1, q, g, some, columns]
                    back[q, g, 0, some, columns] = real * cosine - imag * sine
                    back[q, g, 1, some, columns] = real * sine + imag * cosine
        for partner in partners:
            pltpu.make_async_remote_copy(
                src_ref=back.at[q, partner],
                dst_ref=home.at[q, :, mine, :],
                send_sem=back_send.at[q],
                recv_sem=back_recv.at[q],
                device_id=(az, partner),
                device_id_type=MESH,
            ).start()
        home[q, :, mine, :] = back[q, me]
        return carry

    lax.fori_loop(0, CLASSES, range_work, 0)

    consts[2].wait()
    total[...] = jnp.zeros_like(total)

    def focus(q, carry):
        lot = back.at[q, pl.ds(0, OTHERS)]
        pltpu.make_async_copy(lot, lot, back_recv.at[q]).wait()
        real_high, real_low = split(home[q, 0])
        imag_high, imag_low = split(home[q, 1])
        block_high = jnp.concatenate(
            [
                jnp.concatenate([real_high, imag_high], axis=1),
                jnp.concatenate([-imag_high, real_high], axis=1),
            ],
            axis=0,
        )
        block_low = jnp.concatenate(
            [
                jnp.concatenate([real_low, imag_low], axis=1),
                jnp.concatenate([-imag_low, real_low], axis=1),
            ],
            axis=0,
        )
        total[...] += (
            dot(inverse[q, 0], block_high)
            + dot(inverse[q, 1], block_high)
            + dot(inverse[q, 0], block_low)
        )
        return carry

    lax.fori_loop(0, CLASSES, focus, 0)
    out[0] = total[:, :WIDTH]
    out[1] = total[:, WIDTH:]

    for copy in halo_copies:
        copy.wait_send()

    def drain(q, carry):
        for side in range(2):
            lot = got.at[q, side, pl.ds(0, OTHERS)]
            pltpu.make_async_copy(lot, lot, made_send.at[q, side]).wait()
        lot = back.at[q, pl.ds(0, OTHERS)]
        pltpu.make_async_copy(lot, lot, back_send.at[q]).wait()
        return carry

    lax.fori_loop(0, CLASSES, drain, 0)


def per_device(tables, echo, range_row, aperture, centroid_table, rate_table):
    forward, inverse, dense, twiddle, weights = tables
    vmem = pl.BlockSpec(memory_space=pltpu.VMEM)
    smem = pl.BlockSpec(memory_space=pltpu.SMEM)
    anywhere = pl.BlockSpec(memory_space=pl.ANY)
    semaphore = pltpu.SemaphoreType.DMA
    return pl.pallas_call(
        kernel,
        out_shape=jax.ShapeDtypeStruct((2, SEG, WIDTH), F32),
        in_specs=[vmem, vmem, vmem, vmem, smem, smem, smem, anywhere, anywhere, anywhere],
        out_specs=vmem,
        scratch_shapes=[
            pltpu.VMEM((CLASSES, 2, SEG, 2 * SEG), BF16),
            pltpu.VMEM((CLASSES, 2, SEG, 2 * SEG), BF16),
            pltpu.VMEM((2, 2, 2 * WIDTH, 2 * WIDTH), BF16),
            pltpu.VMEM((2, 4, 2, SEG, HALF), F32),
            pltpu.VMEM((4, 2, SEG, HALF), F32),
            pltpu.VMEM((CLASSES, 2, 2, SEG, HALF), F32),
            pltpu.VMEM((CLASSES, 2, GROUPS, 2, LINES, HALF), F32),
            pltpu.VMEM((CLASSES, GROUPS, 2, LINES, WIDTH), F32),
            pltpu.VMEM((CLASSES, 2, SEG, WIDTH), F32),
            pltpu.VMEM((2, CLASSES, GROUPS, LINES, WIDTH), F32),
            pltpu.VMEM((2, CLASSES, GROUPS, LINES, WIDTH), F32),
            pltpu.VMEM((2, CLASSES, GROUPS, LINES, WIDTH), F32),
            pltpu.VMEM((GROUPS, WIDTH), jnp.int32),
            pltpu.VMEM((GROUPS, WIDTH), F32),
            pltpu.VMEM((2, SEG, 2 * WIDTH), BF16),
            pltpu.VMEM((SEG, 2 * WIDTH), F32),
            pltpu.VMEM((SEG, 2 * WIDTH), F32),
            semaphore((3,)),
            semaphore((2, 4)),
            semaphore((2, 4)),
            semaphore((CLASSES, 2)),
            semaphore((CLASSES, 2)),
            semaphore((CLASSES,)),
            semaphore((CLASSES,)),
        ],
        compiler_params=pltpu.CompilerParams(
            collective_id=0, has_side_effects=True, vmem_limit_bytes=48 * 1024 * 1024
        ),
    )(
        echo,
        range_row.reshape(GROUPS, WIDTH),
        aperture.reshape(GROUPS, WIDTH),
        twiddle,
        centroid_table,
        rate_table,
        weights,
        forward,
        inverse,
        dense,
    )


def solution(mesh):
    forward, inverse = azimuth_tables()
    dense, twiddle = range_tables()
    tables = tuple(
        jnp.asarray(table) for table in (forward, inverse, dense, twiddle, segment_weights())
    )
    in_specs = (P(None, "az", "rg"), P(), P(), P(), P())
    out_specs = P(None, "az", "rg")
    return jax.shard_map(
        partial(per_device, tables),
        mesh=mesh,
        in_specs=in_specs,
        out_specs=out_specs,
        check_vma=False,
    )
```

time: 294 us -> 101 us (0.34)
  the two profiles are of different devices: /device:TPU:27 before, /device:TPU:1 now
where the time goes in v1:
time: 101 us
  Pallas kernels  91.3 us (90%)
  local copies, waits for them, and re-layouts  9.36 us (9%)
    pallas_call x1, Pallas kernels, per_device(): pl.pallas_call(kernel, out_shape=jax.ShapeDtypeStruct((2, SEG, WIDTH), F3...  91.3 us
    unnamed x15, local copies, waits for them, and re-layouts  7.92 us

profile of v1, /device:TPU:1, one launch (start us, length us, event | category | flops | bytes accessed | tf_op | source)
XLA Modules:
  0.0 100.6 jit_solution(17625208933405288890)
XLA Ops:
  0.0 0.7 reshape.6.range_row
  0.7 0.7 reshape.7.aperture
  1.4 0.0 copy-start
  1.4 1.7 %copy-done = bf16[5,2,256,512]{3,2,1,0:T(8,128)(2,1)S(1)} copy-done((bf16[5,2,256,512]{3,2,1,0:T(8,128)(2,1)S(1)}, bf16[5,2,256,512]{3,2,1,0:T(8,128)(2,1)}, u32[]{:S(2)}) %copy-start) | copy-done | bytes 2621464
  3.2 0.0 copy-start.1
  3.2 1.6 %copy-done.1 = bf16[2,2,512,512]{3,2,1,0:T(8,128)(2,1)S(1)} copy-done((bf16[2,2,512,512]{3,2,1,0:T(8,128)(2,1)S(1)}, bf16[2,2,512,512]{3,2,1,0:T(8,128)(2,1)}, u32[]{:S(2)}) %copy-start.1) | copy-done | bytes 2097176
  4.8 0.0 copy-start.2
  4.8 1.0 %copy-done.2 = f32[2,256,256]{2,1,0:T(8,128)S(1)} copy-done((f32[2,256,256]{2,1,0:T(8,128)S(1)}, f32[2,256,256]{2,1,0:T(8,128)}, u32[]{:S(2)}) %copy-start.2) | copy-done | bytes 524312
  5.8 0.0 copy-start.3
  5.8 0.8 copy-done.3
  6.6 0.0 copy-start.4
  6.6 0.7 copy-done.4
  7.3 0.0 copy-start.5
  7.3 0.7 copy-done.5
  7.9 0.0 copy-start.6
  7.9 0.7 copy-done.6
  8.6 91.3 %shard_map.100 = f32[2,256,256]{2,1,0:T(8,128)S(1)} custom-call(f32[2,256,256]{2,1,0:T(8,128)S(1)} %copy-done.2, s32[16,256]{1,0:T(8,128)S(1)} %reshape.6.range_row, s32[16,256]{1,0:T(8,128)S(1)} %reshape.7.aperture, f32[2,16,256]{2,1,0:T(8,128)S(1)} %copy-done.3, s32[64]{0:T(128)S(1)} %copy-done.5, f32[64]{0:T(128)S(1)} %copy-done.6, f32[5,4]{1,0:T(8,128)S(1)} %copy-done.4, ...), custom_call_target="tpu_custom_call" | custom-call | tf_op jit(solution)/shard_map/pallas_call | solution.py:494
  99.9 0.8 copy.12
Async XLA Ops:
  1.4 1.7 %copy-start = (bf16[5,2,256,512]{3,2,1,0:T(8,128)(2,1)S(1)}, bf16[5,2,256,512]{3,2,1,0:T(8,128)(2,1)}, u32[]{:S(2)}) copy-start(bf16[5,2,256,512]{3,2,1,0:T(8,128)(2,1)} %constant.12.clone.forward_hbm) | copy-start | bytes 7864324
  3.2 1.6 %copy-start.1 = (bf16[2,2,512,512]{3,2,1,0:T(8,128)(2,1)S(1)}, bf16[2,2,512,512]{3,2,1,0:T(8,128)(2,1)}, u32[]{:S(2)}) copy-start(bf16[2,2,512,512]{3,2,1,0:T(8,128)(2,1)} %constant.14.clone.range_hbm) | copy-start | bytes 6291460
  4.8 1.0 %copy-start.2 = (f32[2,256,256]{2,1,0:T(8,128)S(1)}, f32[2,256,256]{2,1,0:T(8,128)}, u32[]{:S(2)}) copy-start(f32[2,256,256]{2,1,0:T(8,128)} %echo.1) | copy-start | bytes 1572868
  5.8 0.8 copy-start.3
  6.6 0.7 copy-start.4
  7.3 0.7 copy-start.5
  7.9 0.7 copy-start.6

commit v2 on v1

v2 whole, which is shorter than its diff:
```python
from functools import partial
import math

import jax
import jax.numpy as jnp
import numpy as np
from jax import lax
from jax.experimental import pallas as pl
from jax.experimental.pallas import tpu as pltpu
from jax.sharding import PartitionSpec as P
import ml_dtypes

F32 = jnp.float32
BF16 = jnp.bfloat16
MESH = pl.DeviceIdType.MESH

SEG = 256
CLASSES = 5
LENGTH = SEG * CLASSES
GROUPS = 16
WIDTH = 256
TOTAL = GROUPS * WIDTH
CHIPS = 64
LINES = SEG // CHIPS
ROWS = 2 * LINES
PAIRS = 4
HALF = 128


def links_of(step):
    load = np.zeros(6)
    for axis, hops in enumerate(step[:3]):
        load[2 * axis] += hops in (1, 2)
        load[2 * axis + 1] += hops in (2, 3)
    return load


def spread(steps):
    load, remaining, ordered = np.zeros(6), list(steps), []
    while remaining:
        levels = [
            (np.ptp(load + links_of(step)), -links_of(step).sum(), step) for step in remaining
        ]
        chosen = min(levels)[2]
        ordered.append(chosen)
        remaining.remove(chosen)
        load = load + links_of(chosen)
    return ordered


RING = range(4)
OUTWARD = spread([(dz, dx, dy) for dz in RING for dx in RING for dy in RING])
HOMEWARD = spread(
    [(dz, dx, dy, dc) for dz in RING for dx in (0, 2) for dy in RING for dc in (0, 1)]
)


def pair_split(values):
    high = values.astype(ml_dtypes.bfloat16)
    low = (values - high.astype(np.float64)).astype(ml_dtypes.bfloat16)
    return np.stack([high, low])


def azimuth_tables():
    pulse = np.arange(SEG)
    bins = np.arange(SEG)[None, :] * CLASSES + np.arange(CLASSES)[:, None]
    turns = ((2 * SEG + pulse)[None, :, None] * bins[:, None, :]) % LENGTH
    angle = turns * (2.0 * np.pi / LENGTH)
    scale = 1.0 / math.sqrt(LENGTH)
    cosine, sine = np.cos(angle) * scale, np.sin(angle) * scale
    real = np.stack([cosine, -sine]).reshape(2, CLASSES, SEG, CHIPS, LINES)
    imag = np.stack([sine, cosine]).reshape(2, CLASSES, SEG, CHIPS, LINES)
    inverse = np.stack([real, imag]).transpose(2, 0, 3, 4, 1, 5)
    inverse = inverse.reshape(CLASSES, 2 * SEG, CHIPS * ROWS)
    forward = inverse.transpose(0, 2, 1)
    return pair_split(forward).transpose(1, 0, 2, 3), pair_split(inverse).transpose(1, 0, 2, 3)


def range_tables():
    index = np.arange(WIDTH)
    angle = (index[:, None] * index[None, :] % WIDTH) * (2.0 * np.pi / WIDTH)
    cosine, sine = np.cos(angle), np.sin(angle)
    forward = np.block([[cosine, -sine], [sine, cosine]])
    inverse = np.block([[cosine, sine], [-sine, cosine]])
    fine = np.arange(GROUPS)[:, None] * index[None, :] * (2.0 * np.pi / TOTAL)
    twiddle = np.stack([np.cos(fine), np.sin(fine)]).astype(np.float32)
    return np.stack([pair_split(forward), pair_split(inverse)]), twiddle


WEIGHTS = [
    [
        (math.cos(2.0 * math.pi * q * step / CLASSES), math.sin(2.0 * math.pi * q * step / CLASSES))
        for step in (1, 2)
    ]
    for q in range(CLASSES)
]


def weight(q, step, part):
    value = jnp.float32(WEIGHTS[0][step - 1][part])
    for other in range(1, CLASSES):
        value = jnp.where(q == other, jnp.float32(WEIGHTS[other][step - 1][part]), value)
    return value


def split(value):
    high = value.astype(BF16)
    return high, (value - high.astype(F32)).astype(BF16)


def fitted(function, powers):
    nodes = np.cos((np.arange(400) + 0.5) * np.pi / 400) * 0.5
    nodes = nodes[nodes > 0]
    basis = np.stack([(2 * nodes) ** p for p in powers], axis=1)
    solved = np.linalg.lstsq(basis, function(2.0 * np.pi * nodes), rcond=None)[0]
    return [float(value * 2.0**p) for value, p in zip(solved, powers)]


SINE = fitted(np.sin, [1, 3, 5, 7, 9, 11])
COSINE = fitted(np.cos, [0, 2, 4, 6, 8, 10, 12])


def turn(cycles):
    left = cycles - jnp.floor(cycles + 0.5)
    square = left * left
    sine, cosine = SINE[-1], COSINE[-1]
    for value in SINE[-2::-1]:
        sine = sine * square + value
    for value in COSINE[-2::-1]:
        cosine = cosine * square + value
    return cosine, sine * left


def times_turn(value, quarter):
    real, imag = value
    quarter %= 4
    if quarter == 0:
        return real, imag
    if quarter == 1:
        return -imag, real
    if quarter == 2:
        return -real, -imag
    return imag, -real


def four(values, sign):
    a, b, c, d = values
    ac = (a[0] + c[0], a[1] + c[1])
    am = (a[0] - c[0], a[1] - c[1])
    bd = (b[0] + d[0], b[1] + d[1])
    bm = times_turn((b[0] - d[0], b[1] - d[1]), sign)
    return [
        (ac[0] + bd[0], ac[1] + bd[1]),
        (am[0] + bm[0], am[1] + bm[1]),
        (ac[0] - bd[0], ac[1] - bd[1]),
        (am[0] - bm[0], am[1] - bm[1]),
    ]


def sixteen(values, sign):
    inner = [four(values[low::4], sign) for low in range(4)]
    result = [None] * 16
    for first in range(4):
        column = []
        for low in range(4):
            real, imag = inner[low][first]
            step = low * first
            if step % 4 == 0:
                column.append(times_turn((real, imag), sign * (step // 4)))
            else:
                angle = sign * 2.0 * math.pi * step / 16
                cosine, sine = math.cos(angle), math.sin(angle)
                if step % 2 == 0:
                    root = math.sqrt(0.5)
                    up = 1.0 if cosine > 0 else -1.0
                    side = 1.0 if sine > 0 else -1.0
                    if up == side:
                        column.append(((real - imag) * (up * root), (real + imag) * (up * root)))
                    else:
                        column.append(((real + imag) * (up * root), (imag - real) * (up * root)))
                else:
                    column.append((real * cosine - imag * sine, real * sine + imag * cosine))
        outer = four(column, sign)
        for second in range(4):
            result[first + 4 * second] = outer[second]
    return result


def dot(left, right):
    return jnp.dot(left, right, preferred_element_type=F32)


def kernel(
    echo_hbm,
    range_row_hbm,
    aperture_hbm,
    centroid_hbm,
    rate_hbm,
    forward_hbm,
    inverse_hbm,
    dense_hbm,
    twiddle_hbm,
    out,
    echo,
    pulses,
    range_row,
    aperture,
    centroid_table,
    rate_table,
    forward,
    inverse,
    dense,
    twiddle,
    made,
    got,
    back,
    home,
    one,
    two,
    three,
    centroid,
    rate,
    left,
    mixed,
    total,
    load_sem,
    forward_sem,
    made_send,
    made_recv,
    swap_send,
    swap_recv,
    back_send,
    back_recv,
):
    az = lax.axis_index("az")
    me = lax.axis_index("rg")
    z, x_low = az // 2, az % 2
    x, y, core = (me // 8) * 2 + x_low, (me // 2) % 4, me % 2
    chip = z * 16 + x * 4 + y
    same = x_low == core
    apart = jnp.where(same, 0, 1)
    zs = [(z + step) % 4 for step in RING]
    xs = [(x + step) % 4 for step in RING]
    ys = [(y + step) % 4 for step in RING]
    cores = [core, 1 - core]
    near = {step: (x + apart + step) % 4 for step in (0, 2)}
    far = {step: (x + 1 - apart + step) % 4 for step in (0, 2)}

    def place(z_at, x_at, y_at, core_at):
        return (z_at * 2 + x_at % 2, (x_at // 2) * 8 + y_at * 2 + core_at)

    loads = [
        pltpu.make_async_copy(source, target, load_sem.at[i])
        for i, (source, target) in enumerate(
            (
                (echo_hbm, echo),
                (range_row_hbm, range_row),
                (aperture_hbm, aperture),
                (centroid_hbm, centroid_table),
                (rate_hbm, rate_table),
                (twiddle_hbm, twiddle),
                (dense_hbm, dense),
                (inverse_hbm, inverse),
            )
        )
    ]
    forward_loads = [
        pltpu.make_async_copy(forward_hbm.at[q], forward.at[q], forward_sem.at[q])
        for q in range(CLASSES)
    ]
    for copy in loads[:1] + forward_loads[:1] + loads[1:6] + forward_loads[1:] + loads[6:]:
        copy.start()

    barrier = pltpu.get_barrier_semaphore()

    def greet(target):
        pl.semaphore_signal(barrier, inc=1, device_id=target, device_id_type=MESH)

    for dz, dx, dy, dc in HOMEWARD:
        target = place(zs[dz], near[dx], ys[dy], cores[dc])
        if (dz, dx, dy, dc) == (0, 0, 0, 0):
            pl.when(jnp.logical_not(same))(partial(greet, target))
        else:
            greet(target)
    for dz in RING:
        for dx in (0, 2):
            for dy in RING:
                greet(place(zs[dz], far[dx], ys[dy], x_low))

    loads[0].wait()
    for part in range(2):
        rows = slice(part * SEG, (part + 1) * SEG)
        pulses[0, rows, :], pulses[1, rows, :] = split(echo[part])

    def azimuth(q, carry):
        pltpu.make_async_copy(forward_hbm.at[q], forward.at[q], forward_sem.at[q]).wait()
        spectrum = (
            dot(forward[q, 0], pulses[0])
            + dot(forward[q, 1], pulses[0])
            + dot(forward[q, 0], pulses[1])
        )
        made[q] = spectrum.reshape(CHIPS, ROWS, WIDTH)

        @pl.when(q == 0)
        def _():
            pl.semaphore_wait(barrier, 96 - jnp.where(same, 1, 0))

        for dz, dx, dy in OUTWARD:
            target = place(zs[dz], xs[dx], ys[dy], x_low)
            owner = zs[dz] * 16 + xs[dx] * 4 + ys[dy]

            def send():
                pltpu.make_async_remote_copy(
                    src_ref=made.at[q, owner],
                    dst_ref=got.at[q, x_low, z, me],
                    send_sem=made_send.at[q],
                    recv_sem=made_recv.at[q],
                    device_id=target,
                    device_id_type=MESH,
                ).start()

            def keep():
                pltpu.make_async_copy(
                    made.at[q, owner], got.at[q, x_low, z, me], made_recv.at[q]
                ).start()

            if (dz, dx, dy) == (0, 0, 0):
                pl.when(jnp.logical_not(same))(send)
                pl.when(same)(keep)
            else:
                send()
        return carry

    lax.fori_loop(0, CLASSES, azimuth, 0)

    for copy in loads[1:6]:
        copy.wait()
    for g in range(GROUPS):
        here = pl.ds(g * WIDTH, WIDTH)
        centroid[g : g + 1, :] = range_row[here].reshape(1, WIDTH)
    rows = centroid[...]
    centers = jnp.zeros((GROUPS, WIDTH), jnp.int32)
    rates = jnp.zeros((GROUPS, WIDTH), F32)
    for entry in range(64):
        hit = rows == entry
        centers = jnp.where(hit, centroid_table[entry], centers)
        rates = jnp.where(hit, rate_table[entry], rates)
    centroid[...] = centers
    rate[...] = rates

    lane = lax.broadcasted_iota(jnp.int32, (ROWS, WIDTH), 1)
    line = lax.broadcasted_iota(jnp.int32, (ROWS, WIDTH), 0) % LINES

    def doppler(bins):
        fraction = bins.astype(F32) * (1.0 / LENGTH)
        squared = jnp.maximum(1.0 - 1.5 * fraction * fraction, 0.1)
        migration = jnp.sqrt(squared)
        return squared, migration, 1.0 / migration - 1.0

    def phases(q, carry):
        bins = CLASSES * (LINES * chip + line) + q
        unused, low_migration, low_scaling = doppler(bins)
        unused, high_migration, high_scaling = doppler(bins - LENGTH)
        squared, unused, zero_scaling = doppler(jnp.where(bins < LENGTH // 2, bins, bins - LENGTH))
        square_gain = squared * (150.0 / (TOTAL * TOTAL))
        linear_gain = zero_scaling * 0.05

        def each_group(g, inner):
            here = pl.ds(g, 1)
            center = centroid[here, :]
            time = (g * WIDTH + lane).astype(F32) * (1.0 / TOTAL) + (0.5 / TOTAL - 0.5)
            low = bins <= center + (LENGTH // 2 - 1)
            migration = jnp.where(low, low_migration, high_migration)
            scaling = jnp.where(low, low_scaling, high_scaling)
            offset = jnp.where(low, bins, bins - LENGTH) - center
            lagged = time - 0.2 * scaling
            cosine, sine = turn(-150.0 * scaling * lagged * lagged)
            one[0, q, g] = cosine
            one[1, q, g] = sine
            cosine, sine = turn(
                rate[here, :] * (migration - 1.0) + 150.0 * scaling * (1.0 + scaling) * time * time
            )
            wide = aperture[pl.ds(pl.multiple_of(g * WIDTH, WIDTH), WIDTH)].reshape(1, WIDTH)
            keep = jnp.where(2 * jnp.abs(offset) < wide, 1.0 / TOTAL, 0.0)
            three[0, q, g] = cosine * keep
            three[1, q, g] = sine * keep
            frequency = (GROUPS * lane + g - jnp.where(lane >= HALF, TOTAL, 0)).astype(F32)
            cosine, sine = turn((square_gain * frequency + linear_gain) * frequency)
            two[0, q, g] = cosine
            two[1, q, g] = sine
            return inner

        return lax.fori_loop(0, GROUPS, each_group, carry)

    lax.fori_loop(0, CLASSES, phases, 0)

    sibling = (az, me + 1 - 2 * core)

    def swap(q):
        return pltpu.make_async_remote_copy(
            src_ref=got.at[q, core],
            dst_ref=got.at[q, core],
            send_sem=swap_send.at[q],
            recv_sem=swap_recv.at[q],
            device_id=sibling,
            device_id_type=MESH,
        )

    def arrive(q):
        lot = got.at[q, core]
        pltpu.make_async_copy(lot, lot, made_recv.at[q]).wait()
        swap(q).start()

    upper_rows = lax.broadcasted_iota(jnp.int32, (ROWS, HALF), 0) < LINES
    flip = jnp.where(upper_rows, 1.0, -1.0).astype(F32)
    first_before = core.astype(F32)
    last_after = 1.0 - first_before

    def turned_rows(value):
        return pltpu.roll(value, LINES, 0)

    def range_work(q, carry):
        @pl.when(q < CLASSES - 1)
        def _():
            arrive(q + 1)

        swap(q).wait_recv()
        c_one, s_one = weight(q, 1, 0), weight(q, 1, 1)
        c_two, s_two = weight(q, 2, 0), weight(q, 2, 1)

        def block(segment, g, columns):
            value = got[q, core, segment, g, :, columns]
            before = got[q, 1 - core, jnp.maximum(segment - 1 + core, 0), g, :, columns]
            after = got[q, 1 - core, jnp.minimum(segment + core, 3), g, :, columns]
            if segment == 0:
                before = before * first_before
            if segment == 3:
                after = after * last_after
            value = value + c_one * (after + before)
            side = s_one * (after - before)
            if segment > 0:
                before = got[q, core, segment - 1, g, :, columns]
                value = value + c_two * before
                side = side - s_two * before
            if segment < 3:
                after = got[q, core, segment + 1, g, :, columns]
                value = value + c_two * after
                side = side + s_two * after
            return value + flip * turned_rows(side)

        for upper in range(2):
            for side in range(2):
                columns = slice(side * HALF, (side + 1) * HALF)
                values = []
                for g in range(GROUPS):
                    first, second = (block(2 * upper + i, g, columns) for i in range(2))
                    real = jnp.where(upper_rows, first, turned_rows(second))
                    imag = jnp.where(upper_rows, turned_rows(first), second)
                    cosine, sine = one[0, q, g, :, columns], one[1, q, g, :, columns]
                    values.append((real * cosine - imag * sine, real * sine + imag * cosine))
                values = sixteen(values, -1)
                for g in range(GROUPS):
                    real, imag = values[g]
                    cosine, sine = twiddle[0, g : g + 1, columns], twiddle[1, g : g + 1, columns]
                    values[g] = (real * cosine + imag * sine, imag * cosine - real * sine)
                for g in range(0, GROUPS, 2):
                    spot = slice(upper * HALF + g * 8, upper * HALF + g * 8 + 16)
                    for part in range(2):
                        both = jnp.concatenate([values[g][part], values[g + 1][part]], axis=0)
                        lanes = slice(part * WIDTH + side * HALF, part * WIDTH + (side + 1) * HALF)
                        left[0, spot, lanes], left[1, spot, lanes] = split(both)
        for upper in range(2):
            area = slice(upper * HALF, (upper + 1) * HALF)
            mixed[area, :] = (
                dot(left[0, area, :], dense[0, 0])
                + dot(left[0, area, :], dense[0, 1])
                + dot(left[1, area, :], dense[0, 0])
            )
        for upper in range(2):
            for g in range(0, GROUPS, 2):
                spot = slice(upper * HALF + g * 8, upper * HALF + g * 8 + 16)
                real, imag = mixed[spot, :WIDTH], mixed[spot, WIDTH:]
                cosine = jnp.concatenate([two[0, q, g], two[0, q, g + 1]], axis=0)
                sine = jnp.concatenate([two[1, q, g], two[1, q, g + 1]], axis=0)
                left[0, spot, :WIDTH], left[1, spot, :WIDTH] = split(real * cosine - imag * sine)
                left[0, spot, WIDTH:], left[1, spot, WIDTH:] = split(real * sine + imag * cosine)
        for upper in range(2):
            area = slice(upper * HALF, (upper + 1) * HALF)
            mixed[area, :] = (
                dot(left[0, area, :], dense[1, 0])
                + dot(left[0, area, :], dense[1, 1])
                + dot(left[1, area, :], dense[1, 0])
            )
        for upper in range(2):
            for side in range(2):
                columns = slice(side * HALF, (side + 1) * HALF)
                values = []
                for g in range(GROUPS):
                    spot = slice(upper * HALF + g * 8, upper * HALF + g * 8 + 8)
                    real = mixed[spot, side * HALF : (side + 1) * HALF]
                    imag = mixed[spot, WIDTH + side * HALF : WIDTH + (side + 1) * HALF]
                    cosine, sine = twiddle[0, g : g + 1, columns], twiddle[1, g : g + 1, columns]
                    values.append((real * cosine - imag * sine, real * sine + imag * cosine))
                values = sixteen(values, 1)
                for g in range(GROUPS):
                    real, imag = values[g]
                    cosine, sine = three[0, q, g, :, columns], three[1, q, g, :, columns]
                    real, imag = real * cosine - imag * sine, real * sine + imag * cosine
                    first = 2 * upper * GROUPS + g
                    back[q, first, :, columns] = jnp.where(upper_rows, real, turned_rows(imag))
                    back[q, first + GROUPS, :, columns] = jnp.where(
                        upper_rows, turned_rows(real), imag
                    )
        for dz, dx, dy, dc in HOMEWARD:
            target = place(zs[dz], near[dx], ys[dy], cores[dc])
            piece = zs[dz] * GROUPS + target[1]

            def send():
                pltpu.make_async_remote_copy(
                    src_ref=back.at[q, piece],
                    dst_ref=home.at[q, chip],
                    send_sem=back_send.at[q],
                    recv_sem=back_recv.at[q],
                    device_id=target,
                    device_id_type=MESH,
                ).start()

            def keep():
                pltpu.make_async_copy(
                    back.at[q, piece], home.at[q, chip], back_recv.at[q]
                ).start()

            if (dz, dx, dy, dc) == (0, 0, 0, 0):
                pl.when(jnp.logical_not(same))(send)
                pl.when(same)(keep)
            else:
                send()
        return carry

    arrive(0)
    loads[6].wait()
    lax.fori_loop(0, CLASSES, range_work, 0)

    loads[7].wait()
    total[...] = jnp.zeros_like(total)

    def focus(q, carry):
        lot = home.at[q]
        pltpu.make_async_copy(lot, lot, back_recv.at[q]).wait()
        high, low = split(home[q].reshape(CHIPS * ROWS, WIDTH))
        total[...] += (
            dot(inverse[q, 0], high) + dot(inverse[q, 1], high) + dot(inverse[q, 0], low)
        )
        return carry

    lax.fori_loop(0, CLASSES, focus, 0)
    out[0] = total[:SEG, :]
    out[1] = total[SEG:, :]

    def drain(q, carry):
        swap(q).wait_send()

        @pl.when(same)
        def _():
            for buffer, semaphore in ((made, made_send), (back, back_send)):
                lot = buffer.at[q, pl.ds(0, CHIPS - 1)]
                pltpu.make_async_copy(lot, lot, semaphore.at[q]).wait()

        @pl.when(jnp.logical_not(same))
        def _():
            for buffer, semaphore in ((made, made_send), (back, back_send)):
                lot = buffer.at[q]
                pltpu.make_async_copy(lot, lot, semaphore.at[q]).wait()

        return carry

    lax.fori_loop(0, CLASSES, drain, 0)


def per_device(tables, echo, range_row, aperture, centroid_table, rate_table):
    hbm = pl.BlockSpec(memory_space=pltpu.HBM)
    semaphore = pltpu.SemaphoreType.DMA
    return pl.pallas_call(
        kernel,
        out_shape=jax.ShapeDtypeStruct((2, SEG, WIDTH), F32),
        in_specs=[hbm] * 9,
        out_specs=pl.BlockSpec(memory_space=pltpu.VMEM),
        scratch_shapes=[
            pltpu.VMEM((2, SEG, WIDTH), F32),
            pltpu.VMEM((2, 2 * SEG, WIDTH), BF16),
            pltpu.VMEM((TOTAL,), jnp.int32),
            pltpu.VMEM((TOTAL,), jnp.int32),
            pltpu.SMEM((64,), jnp.int32),
            pltpu.SMEM((64,), F32),
            pltpu.VMEM((CLASSES, 2, 2 * SEG, 2 * SEG), BF16),
            pltpu.VMEM((CLASSES, 2, 2 * SEG, 2 * SEG), BF16),
            pltpu.VMEM((2, 2, 2 * WIDTH, 2 * WIDTH), BF16),
            pltpu.VMEM((2, GROUPS, WIDTH), F32),
            pltpu.VMEM((CLASSES, CHIPS, ROWS, WIDTH), F32),
            pltpu.VMEM((CLASSES, 2, PAIRS, GROUPS, ROWS, WIDTH), F32),
            pltpu.VMEM((CLASSES, CHIPS, ROWS, WIDTH), F32),
            pltpu.VMEM((CLASSES, CHIPS, ROWS, WIDTH), F32),
            pltpu.VMEM((2, CLASSES, GROUPS, ROWS, WIDTH), F32),
            pltpu.VMEM((2, CLASSES, GROUPS, ROWS, WIDTH), F32),
            pltpu.VMEM((2, CLASSES, GROUPS, ROWS, WIDTH), F32),
            pltpu.VMEM((GROUPS, WIDTH), jnp.int32),
            pltpu.VMEM((GROUPS, WIDTH), F32),
            pltpu.VMEM((2, 2 * HALF, 2 * WIDTH), BF16),
            pltpu.VMEM((2 * HALF, 2 * WIDTH), F32),
            pltpu.VMEM((2 * SEG, WIDTH), F32),
            semaphore((8,)),
            semaphore((CLASSES,)),
            semaphore((CLASSES,)),
            semaphore((CLASSES,)),
            semaphore((CLASSES,)),
            semaphore((CLASSES,)),
            semaphore((CLASSES,)),
            semaphore((CLASSES,)),
        ],
        compiler_params=pltpu.CompilerParams(
            collective_id=0, has_side_effects=True, vmem_limit_bytes=52 * 1024 * 1024
        ),
    )(echo, range_row, aperture, centroid_table, rate_table, *tables)


def solution(mesh):
    forward, inverse = azimuth_tables()
    dense, twiddle = range_tables()
    tables = tuple(jnp.asarray(table) for table in (forward, inverse, dense, twiddle))
    in_specs = (P(None, "az", "rg"), P(), P(), P(), P())
    out_specs = P(None, "az", "rg")
    return jax.shard_map(
        partial(per_device, tables),
        mesh=mesh,
        in_specs=in_specs,
        out_specs=out_specs,
        check_vma=False,
    )
```

time: 101 us -> 76.7 us (0.76)
  Pallas kernels: 91.3 us -> 71 us
  local copies, waits for them, and re-layouts: 9.36 us -> 5.34 us
    pallas_call x1, Pallas kernels: 91.3 us -> 71 us  [per_device(): pl.pallas_call(kernel, out_shape=jax.ShapeDtypeStruct((2, SEG, WIDTH), F3...]
    unnamed x15 -> x13, local copies, waits for them, and re-layouts: 7.92 us -> 5.34 us
    reshape x2 -> x0, local copies, waits for them, and re-layouts: 1.44 us -> none  [the longest x1 0.72 us: per_device(): range_row.reshape(GROUPS, WIDTH)]
where the time goes in v2:
time: 76.7 us; the launch traced here: 76.4 us
  Pallas kernels  71 us (93%)
  local copies, waits for them, and re-layouts  5.34 us (7%)
    pallas_call x1, Pallas kernels, per_device(): pl.pallas_call(kernel, out_shape=jax.ShapeDtypeStruct((2, SEG, WIDTH), F3...  71 us
    unnamed x13, local copies, waits for them, and re-layouts  5.34 us

profile of v2, /device:TPU:1, one launch (start us, length us, event | category | flops | bytes accessed | tf_op | source)
XLA Modules:
  0.0 76.4 jit_solution(13602850438359740120)
XLA Ops:
  0.0 0.0 copy-start
  0.0 1.0 %copy-done = f32[2,256,256]{2,1,0:T(8,128)S(1)} copy-done((f32[2,256,256]{2,1,0:T(8,128)S(1)}, f32[2,256,256]{2,1,0:T(8,128)}, u32[]{:S(2)}) %copy-start) | copy-done | bytes 524312
  1.0 0.0 copy-start.1
  1.0 0.8 copy-done.1
  1.8 0.0 copy-start.2
  1.8 0.7 copy-done.2
  2.5 0.0 copy-start.3
  2.5 0.7 copy-done.3
  3.2 0.0 copy-start.4
  3.2 0.7 copy-done.4
  3.9 0.0 copy-start.5
  3.9 0.7 copy-done.5
  4.5 71.0 %shard_map.91 = f32[2,256,256]{2,1,0:T(8,128)S(1)} custom-call(f32[2,256,256]{2,1,0:T(8,128)S(1)} %copy-done, s32[4096]{0:T(1024)S(1)} %copy-done.2, s32[4096]{0:T(1024)S(1)} %copy-done.3, s32[64]{0:T(128)S(1)} %copy-done.4, f32[64]{0:T(128)S(1)} %copy-done.5, bf16[5,2,512,512]{3,2,1,0:T(8,128)(2,1)} %constant.8.clone.forward_hbm, ...), custom_call_target="tpu_custom_call" | custom-call | tf_op jit(solution)/shard_map/pallas_call | solution.py:583
  75.6 0.8 %copy.11 = f32[2,256,256]{2,1,0:T(8,128)} copy(f32[2,256,256]{2,1,0:T(8,128)S(1)} %shard_map.91) | data formatting | bytes 1048576
Async XLA Ops:
  0.0 1.0 %copy-start = (f32[2,256,256]{2,1,0:T(8,128)S(1)}, f32[2,256,256]{2,1,0:T(8,128)}, u32[]{:S(2)}) copy-start(f32[2,256,256]{2,1,0:T(8,128)} %echo_hbm.1) | copy-start | bytes 1572868
  1.0 0.8 copy-start.1
  1.8 0.7 copy-start.2
  2.5 0.7 copy-start.3
  3.2 0.7 copy-start.4
  3.9 0.7 copy-start.5

commit v3 on v2

--- a/solution.py
+++ b/solution.py
@@ -244,7 +244,6 @@
     ys = [(y + step) % 4 for step in RING]
     cores = [core, 1 - core]
     near = {step: (x + apart + step) % 4 for step in (0, 2)}
-    far = {step: (x + 1 - apart + step) % 4 for step in (0, 2)}
 
     def place(z_at, x_at, y_at, core_at):
         return (z_at * 2 + x_at % 2, (x_at // 2) * 8 + y_at * 2 + core_at)
@@ -268,8 +267,8 @@
         pltpu.make_async_copy(forward_hbm.at[q], forward.at[q], forward_sem.at[q])
         for q in range(CLASSES)
     ]
-    for copy in loads[:1] + forward_loads[:1] + loads[1:6] + forward_loads[1:] + loads[6:]:
-        copy.start()
+    loads[0].start()
+    forward_loads[0].start()
 
     barrier = pltpu.get_barrier_semaphore()
 
@@ -282,11 +281,9 @@
             pl.when(jnp.logical_not(same))(partial(greet, target))
         else:
             greet(target)
-    for dz in RING:
-        for dx in (0, 2):
-            for dy in RING:
-                greet(place(zs[dz], far[dx], ys[dy], x_low))
-
+
+    for copy in forward_loads[1:] + loads[1:]:
+        copy.start()
     loads[0].wait()
     for part in range(2):
         rows = slice(part * SEG, (part + 1) * SEG)
@@ -303,7 +300,7 @@
 
         @pl.when(q == 0)
         def _():
-            pl.semaphore_wait(barrier, 96 - jnp.where(same, 1, 0))
+            pl.semaphore_wait(barrier, CHIPS - jnp.where(same, 1, 0))
 
         for dz, dx, dy in OUTWARD:
             target = place(zs[dz], xs[dx], ys[dy], x_low)
@@ -541,40 +538,45 @@
     loads[6].wait()
     lax.fori_loop(0, CLASSES, range_work, 0)
 
+    def drain(buffer, semaphore, q):
+        @pl.when(same)
+        def _():
+            lot = buffer.at[q, pl.ds(0, CHIPS - 1)]
+            pltpu.make_async_copy(lot, lot, semaphore.at[q]).wait()
+
+        @pl.when(jnp.logical_not(same))
+        def _():
+            lot = buffer.at[q]
+            pltpu.make_async_copy(lot, lot, semaphore.at[q]).wait()
+
+    def drain_forward(q, carry):
+        swap(q).wait_send()
+        drain(made, made_send, q)
+        return carry
+
+    lax.fori_loop(0, CLASSES, drain_forward, 0)
+
     loads[7].wait()
-    total[...] = jnp.zeros_like(total)
-
-    def focus(q, carry):
+
+    def focused(q):
         lot = home.at[q]
         pltpu.make_async_copy(lot, lot, back_recv.at[q]).wait()
         high, low = split(home[q].reshape(CHIPS * ROWS, WIDTH))
-        total[...] += (
-            dot(inverse[q, 0], high) + dot(inverse[q, 1], high) + dot(inverse[q, 0], low)
-        )
+        return dot(inverse[q, 0], high) + dot(inverse[q, 1], high) + dot(inverse[q, 0], low)
+
+    total[...] = focused(0)
+
+    def focus(q, carry):
+        total[...] += focused(q)
+        drain(back, back_send, q - 1)
         return carry
 
-    lax.fori_loop(0, CLASSES, focus, 0)
-    out[0] = total[:SEG, :]
-    out[1] = total[SEG:, :]
-
-    def drain(q, carry):
-        swap(q).wait_send()
-
-        @pl.when(same)
-        def _():
-            for buffer, semaphore in ((made, made_send), (back, back_send)):
-                lot = buffer.at[q, pl.ds(0, CHIPS - 1)]
-                pltpu.make_async_copy(lot, lot, semaphore.at[q]).wait()
-
-        @pl.when(jnp.logical_not(same))
-        def _():
-            for buffer, semaphore in ((made, made_send), (back, back_send)):
-                lot = buffer.at[q]
-                pltpu.make_async_copy(lot, lot, semaphore.at[q]).wait()
-
-        return carry
-
-    lax.fori_loop(0, CLASSES, drain, 0)
+    lax.fori_loop(1, CLASSES - 1, focus, 0)
+    drain(back, back_send, CLASSES - 2)
+    result = total[...] + focused(CLASSES - 1)
+    out[0] = result[:SEG, :]
+    out[1] = result[SEG:, :]
+    drain(back, back_send, CLASSES - 1)
 
 
 def per_device(tables, echo, range_row, aperture, centroid_table, rate_table):
@@ -618,7 +620,7 @@
             semaphore((CLASSES,)),
         ],
         compiler_params=pltpu.CompilerParams(
-            collective_id=0, has_side_effects=True, vmem_limit_bytes=52 * 1024 * 1024
+            collective_id=0, has_side_effects=True, vmem_limit_bytes=63 * 1024 * 1024
         ),
     )(echo, range_row, aperture, centroid_table, rate_table, *tables)
 

time: 76.7 us -> 72.8 us (0.949)
  local copies, waits for them, and re-layouts: 5.34 us -> 1.87 us
    unnamed x13 -> x1, local copies, waits for them, and re-layouts: 5.34 us -> 1.87 us
where the time goes in v3:
time: 72.8 us; the launch traced here: 72.6 us
  Pallas kernels  70.7 us (97%)
  local copies, waits for them, and re-layouts  1.87 us (3%)
    pallas_call x1, Pallas kernels, per_device(): pl.pallas_call(kernel, out_shape=jax.ShapeDtypeStruct((2, SEG, WIDTH), F3...  70.7 us
    unnamed x1, local copies, waits for them, and re-layouts  1.87 us

profile of v3, /device:TPU:1, one launch (start us, length us, event | category | flops | bytes accessed | tf_op | source)
XLA Modules:
  0.0 72.6 jit_solution(9536508572840384915)
XLA Ops:
  0.0 70.7 %shard_map.91 = f32[2,256,256]{2,1,0:T(8,128)} custom-call(f32[2,256,256]{2,1,0:T(8,128)} %echo_hbm.1, s32[4096]{0:T(1024)} %range_row_hbm.1, s32[4096]{0:T(1024)} %aperture_hbm.1, s32[64]{0:T(128)} %centroid_hbm.1, f32[64]{0:T(128)} %rate_hbm.1, bf16[5,2,512,512]{3,2,1,0:T(8,128)(2,1)} %constant.8.clone.forward_hbm, ...), custom_call_target="tpu_custom_call" | custom-call | tf_op jit(solution)/shard_map/pallas_call | solution.py:585
  70.7 1.9 %copy.11 = f32[2,256,256]{2,1,0:T(8,128)} copy(f32[2,256,256]{2,1,0:T(8,128)} %shard_map.91) | data formatting | bytes 1048576

commit v4 on v3

--- a/solution.py
+++ b/solution.py
@@ -33,6 +33,10 @@
         load[2 * axis] += hops in (1, 2)
         load[2 * axis + 1] += hops in (2, 3)
     return load
+
+
+def hops(step):
+    return sum(min(count, 4 - count) for count in step[:3])
 
 
 def spread(steps):
@@ -275,7 +279,7 @@
     def greet(target):
         pl.semaphore_signal(barrier, inc=1, device_id=target, device_id_type=MESH)
 
-    for dz, dx, dy, dc in HOMEWARD:
+    for dz, dx, dy, dc in sorted(HOMEWARD, key=hops, reverse=True):
         target = place(zs[dz], near[dx], ys[dy], cores[dc])
         if (dz, dx, dy, dc) == (0, 0, 0, 0):
             pl.when(jnp.logical_not(same))(partial(greet, target))
@@ -584,7 +588,7 @@
     semaphore = pltpu.SemaphoreType.DMA
     return pl.pallas_call(
         kernel,
-        out_shape=jax.ShapeDtypeStruct((2, SEG, WIDTH), F32),
+        out_shape=pltpu.VMEM((2, SEG, WIDTH), F32),
         in_specs=[hbm] * 9,
         out_specs=pl.BlockSpec(memory_space=pltpu.VMEM),
         scratch_shapes=[
@@ -620,9 +624,14 @@
             semaphore((CLASSES,)),
         ],
         compiler_params=pltpu.CompilerParams(
-            collective_id=0, has_side_effects=True, vmem_limit_bytes=63 * 1024 * 1024
+            collective_id=0, has_side_effects=True, vmem_limit_bytes=52 * 1024 * 1024
         ),
-    )(echo, range_row, aperture, centroid_table, rate_table, *tables)
+    )(
+        *(
+            pltpu.with_memory_space_constraint(operand, pltpu.HBM)
+            for operand in (echo, range_row, aperture, centroid_table, rate_table, *tables)
+        )
+    )
 
 
 def solution(mesh):

time: 72.8 us -> 70.6 us (0.970)
  local copies, waits for them, and re-layouts: 1.87 us -> 0.8 us
  Pallas kernels: 70.7 us -> 69.7 us
    unnamed x1, local copies, waits for them, and re-layouts: 1.87 us -> 0.8 us
    pallas_call x1, Pallas kernels: 70.7 us -> 69.7 us  [per_device(): pl.pallas_call(kernel, out_shape=pltpu.VMEM((2, SEG, WIDTH), F32), in_spe...]
where the time goes in v4:
time: 70.6 us; the launch traced here: 70.5 us
  Pallas kernels  69.7 us (99%)
  local copies, waits for them, and re-layouts  0.8 us (1%)
    pallas_call x1, Pallas kernels, per_device(): pl.pallas_call(kernel, out_shape=pltpu.VMEM((2, SEG, WIDTH), F32), in_spe...  69.7 us

profile of v4, /device:TPU:1, one launch (start us, length us, event | category | flops | bytes accessed | tf_op | source)
XLA Modules:
  0.0 70.5 jit_solution(15778130100272829656)
XLA Ops:
  0.0 69.7 %shard_map.91 = f32[2,256,256]{2,1,0:T(8,128)S(1)} custom-call(f32[2,256,256]{2,1,0:T(8,128)} %echo_hbm.1, s32[4096]{0:T(1024)} %range_row_hbm.1, s32[4096]{0:T(1024)} %aperture_hbm.1, s32[64]{0:T(128)} %centroid_hbm.1, f32[64]{0:T(128)} %rate_hbm.1, bf16[5,2,512,512]{3,2,1,0:T(8,128)(2,1)} %constant.8.clone.forward_hbm, ...), custom_call_target="tpu_custom_call" | custom-call | tf_op jit(solution)/shard_map/pallas_call | solution.py:589
  69.7 0.8 %copy.11 = f32[2,256,256]{2,1,0:T(8,128)} copy(f32[2,256,256]{2,1,0:T(8,128)S(1)} %shard_map.91) | data formatting | bytes 1048576

commit v5 on v4

--- a/solution.py
+++ b/solution.py
@@ -204,7 +204,9 @@
     inverse_hbm,
     dense_hbm,
     twiddle_hbm,
-    out,
+    total,
+    last,
+    last_table,
     echo,
     pulses,
     range_row,
@@ -226,7 +228,6 @@
     rate,
     left,
     mixed,
-    total,
     load_sem,
     forward_sem,
     made_send,
@@ -264,6 +265,7 @@
                 (twiddle_hbm, twiddle),
                 (dense_hbm, dense),
                 (inverse_hbm, inverse),
+                (inverse_hbm.at[CLASSES - 1], last_table),
             )
         )
     ]
@@ -562,10 +564,15 @@
 
     loads[7].wait()
 
-    def focused(q):
+    loads[8].wait()
+
+    def received(q):
         lot = home.at[q]
         pltpu.make_async_copy(lot, lot, back_recv.at[q]).wait()
-        high, low = split(home[q].reshape(CHIPS * ROWS, WIDTH))
+        return split(home[q].reshape(CHIPS * ROWS, WIDTH))
+
+    def focused(q):
+        high, low = received(q)
         return dot(inverse[q, 0], high) + dot(inverse[q, 1], high) + dot(inverse[q, 0], low)
 
     total[...] = focused(0)
@@ -577,20 +584,39 @@
 
     lax.fori_loop(1, CLASSES - 1, focus, 0)
     drain(back, back_send, CLASSES - 2)
-    result = total[...] + focused(CLASSES - 1)
-    out[0] = result[:SEG, :]
-    out[1] = result[SEG:, :]
+    last[0], last[1] = received(CLASSES - 1)
     drain(back, back_send, CLASSES - 1)
+
+
+def finish(total, last, table, out, result, sent):
+    copies = []
+    for block in range(4):
+        rows = slice(block * HALF, (block + 1) * HALF)
+        result[block] = total[rows, :] + (
+            dot(table[0, rows, :], last[0])
+            + dot(table[1, rows, :], last[0])
+            + dot(table[0, rows, :], last[1])
+        )
+        place = out.at[block // 2, pl.ds(block % 2 * HALF, HALF), :]
+        copy = pltpu.make_async_copy(result.at[block], place, sent.at[block])
+        copy.start()
+        copies.append(copy)
+    for copy in copies:
+        copy.wait()
 
 
 def per_device(tables, echo, range_row, aperture, centroid_table, rate_table):
     hbm = pl.BlockSpec(memory_space=pltpu.HBM)
     semaphore = pltpu.SemaphoreType.DMA
-    return pl.pallas_call(
+    parts = pl.pallas_call(
         kernel,
-        out_shape=pltpu.VMEM((2, SEG, WIDTH), F32),
+        out_shape=[
+            pltpu.VMEM((2 * SEG, WIDTH), F32),
+            pltpu.VMEM((2, CHIPS * ROWS, WIDTH), BF16),
+            pltpu.VMEM((2, 2 * SEG, CHIPS * ROWS), BF16),
+        ],
         in_specs=[hbm] * 9,
-        out_specs=pl.BlockSpec(memory_space=pltpu.VMEM),
+        out_specs=[pl.BlockSpec(memory_space=pltpu.VMEM)] * 3,
         scratch_shapes=[
             pltpu.VMEM((2, SEG, WIDTH), F32),
             pltpu.VMEM((2, 2 * SEG, WIDTH), BF16),
@@ -613,8 +639,7 @@
             pltpu.VMEM((GROUPS, WIDTH), F32),
             pltpu.VMEM((2, 2 * HALF, 2 * WIDTH), BF16),
             pltpu.VMEM((2 * HALF, 2 * WIDTH), F32),
-            pltpu.VMEM((2 * SEG, WIDTH), F32),
-            semaphore((8,)),
+            semaphore((9,)),
             semaphore((CLASSES,)),
             semaphore((CLASSES,)),
             semaphore((CLASSES,)),
@@ -632,6 +657,14 @@
             for operand in (echo, range_row, aperture, centroid_table, rate_table, *tables)
         )
     )
+    return pl.pallas_call(
+        finish,
+        out_shape=jax.ShapeDtypeStruct((2, SEG, WIDTH), F32),
+        in_specs=[pl.BlockSpec(memory_space=pltpu.VMEM)] * 3,
+        out_specs=pl.BlockSpec(memory_space=pl.ANY),
+        scratch_shapes=[pltpu.VMEM((4, HALF, WIDTH), F32), semaphore((4,))],
+        compiler_params=pltpu.CompilerParams(vmem_limit_bytes=16 * 1024 * 1024),
+    )(*(pltpu.with_memory_space_constraint(part, pltpu.VMEM) for part in parts))
 
 
 def solution(mesh):

time: 70.6 us -> 70.7 us (level)
  Pallas kernels: 69.7 us -> 70.6 us
  local copies, waits for them, and re-layouts: 0.8 us -> 0 us
    pallas_call x1 -> x2, Pallas kernels: 69.7 us -> 70.6 us  [the longest x1 69.2 us: per_device(): pl.pallas_call(kernel, out_shape=[pltpu.VMEM((2 * SEG, WIDTH), F32), pltp...]
    unnamed x1 -> x0, local copies, waits for them, and re-layouts: 0.8 us -> none
where the time goes in v5:
time: 70.7 us; the launch traced here: 70.6 us
  Pallas kernels  70.6 us (100%)
    pallas_call x1, Pallas kernels, per_device(): pl.pallas_call(kernel, out_shape=[pltpu.VMEM((2 * SEG, WIDTH), F32), pltp...  69.2 us

profile of v5, /device:TPU:1, one launch (start us, length us, event | category | flops | bytes accessed | tf_op | source)
XLA Modules:
  0.0 70.6 jit_solution(4375277622704566209)
XLA Ops:
  0.0 69.2 %shard_map.91 = (f32[512,256]{1,0:T(8,128)S(1)}, bf16[2,512,256]{2,1,0:T(8,128)(2,1)S(1)}, bf16[2,512,512]{2,1,0:T(8,128)(2,1)S(1)}) custom-call(f32[2,256,256]{2,1,0:T(8,128)} %echo_hbm.1, s32[4096]{0:T(1024)} %range_row_hbm.1, s32[4096]{0:T(1024)} %aperture_hbm.1, s32[64]{0:T(128)} %centroid_hbm.1, f32[64]{0:T(128)} %rate_hbm.1, ...), custom_call_target="tpu_custom_call" | custom-call | tf_op jit(solution)/shard_map/pallas_call | solution.py:611
  69.3 1.3 %shard_map.92 = f32[2,256,256]{2,1,0:T(8,128)} custom-call(f32[512,256]{1,0:T(8,128)S(1)} %get-tuple-element.8.total, bf16[2,512,256]{2,1,0:T(8,128)(2,1)S(1)} %get-tuple-element.9.last, bf16[2,512,512]{2,1,0:T(8,128)(2,1)S(1)} %get-tuple-element.10.table), custom_call_target="tpu_custom_call" | custom-call | tf_op jit(solution)/shard_map/pallas_call | solution.py:660

commit v6 on v4

--- a/solution.py
+++ b/solution.py
@@ -243,7 +243,8 @@
     chip = z * 16 + x * 4 + y
     same = x_low == core
     apart = jnp.where(same, 0, 1)
-    zs = [(z + step) % 4 for step in RING]
+    zs = [(z + step + 2 * core) % 4 for step in RING]
+    own_plane = [jnp.logical_and(same, core == side) for side in range(2)]
     xs = [(x + step) % 4 for step in RING]
     ys = [(y + step) % 4 for step in RING]
     cores = [core, 1 - core]
@@ -281,8 +282,8 @@
 
     for dz, dx, dy, dc in sorted(HOMEWARD, key=hops, reverse=True):
         target = place(zs[dz], near[dx], ys[dy], cores[dc])
-        if (dz, dx, dy, dc) == (0, 0, 0, 0):
-            pl.when(jnp.logical_not(same))(partial(greet, target))
+        if (dx, dy, dc) == (0, 0, 0) and dz in (0, 2):
+            pl.when(jnp.logical_not(own_plane[dz // 2]))(partial(greet, target))
         else:
             greet(target)
 
@@ -325,9 +326,9 @@
                     made.at[q, owner], got.at[q, x_low, z, me], made_recv.at[q]
                 ).start()
 
-            if (dz, dx, dy) == (0, 0, 0):
-                pl.when(jnp.logical_not(same))(send)
-                pl.when(same)(keep)
+            if (dx, dy) == (0, 0) and dz in (0, 2):
+                pl.when(jnp.logical_not(own_plane[dz // 2]))(send)
+                pl.when(own_plane[dz // 2])(keep)
             else:
                 send()
         return carry
@@ -531,9 +532,9 @@
                     back.at[q, piece], home.at[q, chip], back_recv.at[q]
                 ).start()
 
-            if (dz, dx, dy, dc) == (0, 0, 0, 0):
-                pl.when(jnp.logical_not(same))(send)
-                pl.when(same)(keep)
+            if (dx, dy, dc) == (0, 0, 0) and dz in (0, 2):
+                pl.when(jnp.logical_not(own_plane[dz // 2]))(send)
+                pl.when(own_plane[dz // 2])(keep)
             else:
                 send()
         return carry

time: 70.6 us -> 70.6 us (level)
  no operation moved by 1% of the time
where the time goes in v6:
time: 70.6 us; the launch traced here: 70.5 us
  Pallas kernels  69.7 us (99%)
  local copies, waits for them, and re-layouts  0.8 us (1%)
    pallas_call x1, Pallas kernels, per_device(): pl.pallas_call(kernel, out_shape=pltpu.VMEM((2, SEG, WIDTH), F32), in_spe...  69.7 us

profile of v6, /device:TPU:1, one launch (start us, length us, event | category | flops | bytes accessed | tf_op | source)
XLA Modules:
  0.0 70.5 jit_solution(11773193874334153251)
XLA Ops:
  0.0 69.7 %shard_map.91 = f32[2,256,256]{2,1,0:T(8,128)S(1)} custom-call(f32[2,256,256]{2,1,0:T(8,128)} %echo_hbm.1, s32[4096]{0:T(1024)} %range_row_hbm.1, s32[4096]{0:T(1024)} %aperture_hbm.1, s32[64]{0:T(128)} %centroid_hbm.1, f32[64]{0:T(128)} %rate_hbm.1, bf16[5,2,512,512]{3,2,1,0:T(8,128)(2,1)} %constant.8.clone.forward_hbm, ...), custom_call_target="tpu_custom_call" | custom-call | tf_op jit(solution)/shard_map/pallas_call | solution.py:590
  69.7 0.8 %copy.11 = f32[2,256,256]{2,1,0:T(8,128)} copy(f32[2,256,256]{2,1,0:T(8,128)S(1)} %shard_map.91) | data formatting | bytes 1048576

commit v7 on v4

--- a/solution.py
+++ b/solution.py
@@ -227,6 +227,7 @@
     left,
     mixed,
     total,
+    both_sem,
     load_sem,
     forward_sem,
     made_send,
@@ -275,19 +276,22 @@
     forward_loads[0].start()
 
     barrier = pltpu.get_barrier_semaphore()
+    sibling = (az, me + 1 - 2 * core)
+    told = lax.rem(y, 2)
 
     def greet(target):
         pl.semaphore_signal(barrier, inc=1, device_id=target, device_id_type=MESH)
 
+    own_turn = jnp.logical_and(same, told == core)
     for dz, dx, dy, dc in sorted(HOMEWARD, key=hops, reverse=True):
-        target = place(zs[dz], near[dx], ys[dy], cores[dc])
-        if (dz, dx, dy, dc) == (0, 0, 0, 0):
-            pl.when(jnp.logical_not(same))(partial(greet, target))
-        else:
-            greet(target)
-
-    for copy in forward_loads[1:] + loads[1:]:
-        copy.start()
+        if dc == 0:
+            target = place(zs[dz], near[dx], ys[dy], told)
+            if (dz, dx, dy) == (0, 0, 0):
+                pl.when(jnp.logical_not(own_turn))(partial(greet, target))
+            else:
+                greet(target)
+    greet(sibling)
+
     loads[0].wait()
     for part in range(2):
         rows = slice(part * SEG, (part + 1) * SEG)
@@ -304,7 +308,9 @@
 
         @pl.when(q == 0)
         def _():
-            pl.semaphore_wait(barrier, CHIPS - jnp.where(same, 1, 0))
+            pl.semaphore_wait(barrier, CHIPS // 2 + 1 - jnp.where(own_turn, 1, 0))
+            pl.semaphore_signal(both_sem, inc=1, device_id=sibling, device_id_type=MESH)
+            pl.semaphore_wait(both_sem, 1)
 
         for dz, dx, dy in OUTWARD:
             target = place(zs[dz], xs[dx], ys[dy], x_low)
@@ -330,6 +336,12 @@
                 pl.when(same)(keep)
             else:
                 send()
+
+        @pl.when(q == 0)
+        def _():
+            for copy in forward_loads[1:] + loads[1:]:
+                copy.start()
+
         return carry
 
     lax.fori_loop(0, CLASSES, azimuth, 0)
@@ -394,8 +406,6 @@
         return lax.fori_loop(0, GROUPS, each_group, carry)
 
     lax.fori_loop(0, CLASSES, phases, 0)
-
-    sibling = (az, me + 1 - 2 * core)
 
     def swap(q):
         return pltpu.make_async_remote_copy(
@@ -614,6 +624,7 @@
             pltpu.VMEM((2, 2 * HALF, 2 * WIDTH), BF16),
             pltpu.VMEM((2 * HALF, 2 * WIDTH), F32),
             pltpu.VMEM((2 * SEG, WIDTH), F32),
+            pltpu.SemaphoreType.REGULAR,
             semaphore((8,)),
             semaphore((CLASSES,)),
             semaphore((CLASSES,)),

time: 70.6 us -> 70.9 us (level)
  no operation moved by 1% of the time
where the time goes in v7:
time: 70.9 us; the launch traced here: 70.8 us
  Pallas kernels  70 us (99%)
  local copies, waits for them, and re-layouts  0.8 us (1%)
    pallas_call x1, Pallas kernels, per_device(): pl.pallas_call(kernel, out_shape=pltpu.VMEM((2, SEG, WIDTH), F32), in_spe...  70 us

profile of v7, /device:TPU:1, one launch (start us, length us, event | category | flops | bytes accessed | tf_op | source)
XLA Modules:
  0.0 70.8 jit_solution(14867915159922618846)
XLA Ops:
  0.0 70.0 %shard_map.91 = f32[2,256,256]{2,1,0:T(8,128)S(1)} custom-call(f32[2,256,256]{2,1,0:T(8,128)} %echo_hbm.1, s32[4096]{0:T(1024)} %range_row_hbm.1, s32[4096]{0:T(1024)} %aperture_hbm.1, s32[64]{0:T(128)} %centroid_hbm.1, f32[64]{0:T(128)} %rate_hbm.1, bf16[5,2,512,512]{3,2,1,0:T(8,128)(2,1)} %constant.8.clone.forward_hbm, ...), custom_call_target="tpu_custom_call" | custom-call | tf_op jit(solution)/shard_map/pallas_call | solution.py:599
  70.0 0.8 %copy.11 = f32[2,256,256]{2,1,0:T(8,128)} copy(f32[2,256,256]{2,1,0:T(8,128)S(1)} %shard_map.91) | data formatting | bytes 1048576

commit v8 on v4

--- a/solution.py
+++ b/solution.py
@@ -43,7 +43,7 @@
     load, remaining, ordered = np.zeros(6), list(steps), []
     while remaining:
         levels = [
-            (np.ptp(load + links_of(step)), -links_of(step).sum(), step) for step in remaining
+            (-hops(step), np.ptp(load + links_of(step)), step) for step in remaining
         ]
         chosen = min(levels)[2]
         ordered.append(chosen)
@@ -286,8 +286,6 @@
         else:
             greet(target)
 
-    for copy in forward_loads[1:] + loads[1:]:
-        copy.start()
     loads[0].wait()
     for part in range(2):
         rows = slice(part * SEG, (part + 1) * SEG)
@@ -330,6 +328,12 @@
                 pl.when(same)(keep)
             else:
                 send()
+
+        @pl.when(q == 0)
+        def _():
+            for copy in forward_loads[1:] + loads[1:]:
+                copy.start()
+
         return carry
 
     lax.fori_loop(0, CLASSES, azimuth, 0)

time: 70.6 us -> 70.5 us (level)
  no operation moved by 1% of the time
where the time goes in v8:
time: 70.5 us; the launch traced here: 70.3 us
  Pallas kernels  69.5 us (99%)
  local copies, waits for them, and re-layouts  0.8 us (1%)
    pallas_call x1, Pallas kernels, per_device(): pl.pallas_call(kernel, out_shape=pltpu.VMEM((2, SEG, WIDTH), F32), in_spe...  69.5 us

profile of v8, /device:TPU:1, one launch (start us, length us, event | category | flops | bytes accessed | tf_op | source)
XLA Modules:
  0.0 70.3 jit_solution(7658801351896133200)
XLA Ops:
  0.0 69.5 %shard_map.91 = f32[2,256,256]{2,1,0:T(8,128)S(1)} custom-call(f32[2,256,256]{2,1,0:T(8,128)} %echo_hbm.1, s32[4096]{0:T(1024)} %range_row_hbm.1, s32[4096]{0:T(1024)} %aperture_hbm.1, s32[64]{0:T(128)} %centroid_hbm.1, f32[64]{0:T(128)} %rate_hbm.1, bf16[5,2,512,512]{3,2,1,0:T(8,128)(2,1)} %constant.8.clone.forward_hbm, ...), custom_call_target="tpu_custom_call" | custom-call | tf_op jit(solution)/shard_map/pallas_call | solution.py:593
  69.5 0.8 %copy.11 = f32[2,256,256]{2,1,0:T(8,128)} copy(f32[2,256,256]{2,1,0:T(8,128)S(1)} %shard_map.91) | data formatting | bytes 1048576
